TPU v7x, 128 devices: a whole 4x4x4 slice. The times are simulated.
128 devices in a mesh: row: 8 (over x, core), col: 16 (over z, y).
Axes of the slice: x: 4, y: 4, z: 4, core: 2. Of those that a mesh axis runs over, the one named last changes fastest.
Arguments:
- matrix: float32 [12288, 24576], P('row', 'col'), may hold values from -6 to 6
- far_diag: float32 [8, 1536], P('row'), may hold values from -6 to 6
- vectors: float32 [24576, 128], P(('row', 'col'))
- factors: float32 [128, 128], replicated, may hold values from -0.5 to 0.5
Outputs:
- updated: float32 [12288, 24576], P('row', 'col')
- far_updated: float32 [8, 1536], P('row')
All inputs are finite; a program needn't handle non-finite values.
Results may differ from a plain program's by a relative error of at most 0.0003.
Values sent between devices are 32-bit elements; how exact they have to be, the bound alone decides.
A program may use at most 128 MiB of HBM per device.

v0:
```python
import jax
import jax.numpy as jnp
from jax import lax
from jax.sharding import PartitionSpec as P


def product(left, right):
    return jnp.dot(left, right, preferred_element_type=jnp.float32, precision=lax.Precision.HIGHEST)


def sym_pair(block, low_diag):
    lower_part = jnp.tril(block)
    lead_full = lower_part + jnp.tril(block, -1).T
    upper_part = jnp.triu(block, 1)
    other_full = upper_part + upper_part.T + jnp.diag(low_diag)
    return (lead_full, other_full)


def body(matrix, far_diag, vectors, factors):
    tile_size = matrix.shape[0]
    grid_count = lax.axis_size("col")
    row_at = lax.axis_index("row")
    col_at = lax.axis_index("col")
    far_row = grid_count - 1 - row_at
    lead = jnp.where(col_at <= row_at, row_at, far_row)
    other = jnp.where(
        col_at < row_at, col_at, jnp.where(col_at == row_at, far_row, col_at - row_at - 1)
    )
    on_diag = col_at == row_at
    low_diag = far_diag[0]

    def pick_tile(whole, index):
        return lax.dynamic_slice_in_dim(whole, index * tile_size, tile_size, 0)

    v_whole = lax.all_gather(vectors, ("row", "col"), axis=0, tiled=True)
    v_lead = pick_tile(v_whole, lead)
    v_other = pick_tile(v_whole, other)
    v_far = pick_tile(v_whole, far_row)

    def diag_terms(operand):
        lead_full, other_full = sym_pair(matrix, low_diag)
        return (product(lead_full, v_lead), product(other_full, v_other))

    def plain_terms(operand):
        return (product(matrix, v_other), product(matrix.T, v_lead))

    z_lead, z_other = lax.cond(on_diag, diag_terms, plain_terms, 0)
    partial_value = jnp.zeros((grid_count * tile_size, vectors.shape[1]), jnp.float32)
    partial_value = lax.dynamic_update_slice_in_dim(partial_value, z_lead, lead * tile_size, 0)
    partial_value = lax.dynamic_update_slice_in_dim(partial_value, z_other, other * tile_size, 0)
    z_piece = lax.psum_scatter(partial_value, ("row", "col"), scatter_dimension=0, tiled=True)
    gram_sum = lax.psum(product(vectors.T, z_piece), ("row", "col"))
    middle = product(product(factors.T, gram_sum), factors)
    w_piece = product(z_piece, factors) - 0.5 * product(vectors, middle)
    w_whole = lax.all_gather(w_piece, ("row", "col"), axis=0, tiled=True)
    w_lead = pick_tile(w_whole, lead)
    w_other = pick_tile(w_whole, other)
    w_far = pick_tile(w_whole, far_row)

    def change(v_one, w_one, v_two, w_two):
        left = jnp.concatenate([v_one, w_one], axis=1)
        right = jnp.concatenate([w_two, v_two], axis=1)
        return product(left, right.T)

    def diag_update(operand):
        lead_full, other_full = sym_pair(matrix, low_diag)
        lead_new = lead_full - change(v_lead, w_lead, v_lead, w_lead)
        other_new = other_full - change(v_other, w_other, v_other, w_other)
        return jnp.tril(lead_new) + jnp.triu(other_new, 1)

    def plain_update(operand):
        return matrix - change(v_lead, w_lead, v_other, w_other)

    updated = lax.cond(on_diag, diag_update, plain_update, 0)
    far_updated = far_diag - 2.0 * jnp.sum(v_far * w_far, axis=1)[None, :]
    return (updated, far_updated)


def solution(mesh):
    in_specs = (P("row", "col"), P("row", None), P(("row", "col"), None), P())
    out_specs = (P("row", "col"), P("row", None))
    return jax.shard_map(body, mesh=mesh, in_specs=in_specs, out_specs=out_specs, check_vma=False)
```

profile of v0, /device:TPU:0, one launch (start us, length us, event | category | flops | bytes accessed | tf_op | source)
XLA Modules:
  0.0 674.4 jit_solution(17753954879929366815)
XLA Ops:
  7.2 0.0 copy-start
  7.2 0.0 all-gather.3.cloned.1.call-start
  7.2 0.7 all-gather.3.cloned.1.call-update
  7.9 0.0 reduce-scatter.2.cloned.1.call-start
  8.0 0.7 reduce
  8.7 78.2 %all-gather.3.cloned.1.call-done = f32[24576,128]{1,0:T(8,128)} async-done(((f32[192,128]{1,0:T(8,128)}), f32[24576,128]{1,0:T(8,128)}) %all-gather.3.cloned.1.call-update) | async-done | bytes 12582928 | tf_op jit(solution)/shard_map/all_gather | solution.py:35
  86.9 1.5 constant_dynamic-slice_fusion.2
  88.4 75.0 %conditional.2 = (f32[1536,128]{1,0:T(8,128)S(1)}, f32[1536,128]{1,0:T(8,128)S(1)}) conditional(s32[]{:T(128)} %convert_element_type.4, (f32[1536,1536]{1,0:T(8,128)}, f32[1536,128]{1,0:T(8,128)S(1)}, f32[1536,128]{1,0:T(8,128)S(1)}) %tuple.22, (f32[1536,1536]{1,0:T(8,128)}, f32[1536,128]{1,0:T(8,128)S(1)}, f32[1536]{0:T(1024)S(1)}, ...), branch_computations={%region_0.1_spmd, %region_1.2_spmd} | conditional | flops 7273711104 | bytes 144721968 | solution.py:47
  97.3 2.1 iota_compare_fusion.2
  99.4 6.2 copy.8
  105.6 9.6 %copy.13 = f32[1536,1536]{0,1:T(8,128)} copy(f32[1536,1536]{1,0:T(8,128)} %get-tuple-element.63) | data formatting | bytes 18874368 | tf_op jit(solution)/shard_map
  115.2 0.0 copy-start.2
  115.2 12.6 %fusion.3 = f32[1536,128]{1,0:T(8,128)S(1)} fusion(f32[1536,128]{1,0:T(8,128)S(1)} %get-tuple-element.43, f32[1536,1536]{0,1:T(8,128)} %copy.13, f32[1536,1536]{1,0:T(8,128)} %get-tuple-element.63, s32[1536]{0:T(1024)S(1)} %iota_add_fusion), kind=kOutput, calls=%fused_computation.4 | convolution fusion | flops 3635675136 | bytes 20453376 | tf_op jit(solution)/shard_map/cond/branch_1_fun/dot_general | solution.py:8
  127.8 0.0 copy-done.2
  127.8 6.9 %broadcast_select_fusion = f32[1536,1536]{0,1:T(8,128)} fusion(pred[1536,1536]{0,1:T(8,128)(4,1)} %copy.8, f32[1536,1536]{0,1:T(8,128)S(1)} %copy-done.2), kind=kLoop, calls=%fused_computation.14 | loop fusion | flops 2359296 | bytes 21233664 | tf_op jit(solution)/shard_map/cond/branch_1_fun/jit(triu)/select_n | solution.py:14
  134.8 9.6 %copy.9 = f32[1536,1536]{1,0:T(8,128)} copy(f32[1536,1536]{0,1:T(8,128)} %broadcast_select_fusion) | data formatting | bytes 18874368 | tf_op jit(solution)/shard_map/cond/branch_1_fun/jit(triu)/select_n | solution.py:14
  144.4 18.8 %fusion.1 = f32[1536,128]{1,0:T(8,128)S(1)} fusion(f32[1536,128]{1,0:T(8,128)S(1)} %get-tuple-element.45, f32[1536,1536]{0,1:T(8,128)} %broadcast_select_fusion, f32[1536,1536]{1,0:T(8,128)} %copy.9, f32[1536]{0:T(1024)S(1)} %get-tuple-element.44), kind=kOutput, calls=%fused_computation.2 | convolution fusion | flops 3633315840 | bytes 20453376 | tf_op jit(solution)/shard_map/cond/branch_1_fun/dot_general | solution.py:8
  163.4 4.8 broadcast_in_dim.42
  168.1 0.0 copy-start.4
  168.1 1.0 constant_dynamic-update-slice_fusion.1
  169.1 1.0 constant_dynamic-update-slice_fusion
  170.1 0.0 copy-start.5
  170.1 0.0 reduce-scatter.2.cloned.1.call-update
  170.2 0.0 all-reduce.2.cloned.1.call-start
  170.2 219.9 %reduce-scatter.2.cloned.1.call-done = f32[192,128]{1,0:T(8,128)} async-done(((f32[24576,128]{1,0:T(8,128)}), f32[192,128]{1,0:T(8,128)}) %reduce-scatter.2.cloned.1.call-update) | async-done | bytes 98320 | tf_op jit(solution)/shard_map/reduce_scatter | solution.py:51
  390.1 0.0 copy-done.4
  390.1 2.0 convolution_bitcast_fusion
  392.1 0.0 all-reduce.2.cloned.1.call-update
  392.1 0.0 all-gather.5.cloned.1.call-start
  392.1 0.0 copy-done
  392.1 1.1 fusion.44
  393.3 134.9 %all-reduce.2.cloned.1.call-done = f32[128,128]{0,1:T(8,128)} async-done(((f32[128,128]{0,1:T(8,128)}), f32[128,128]{0,1:T(8,128)}) %all-reduce.2.cloned.1.call-update) | async-done | bytes 65552 | tf_op jit(solution)/shard_map/psum | solution.py:52
  528.1 1.0 fusion.45
  529.2 0.3 fusion.46
  529.5 0.9 fusion.41
  530.4 0.0 all-gather.5.cloned.1.call-update
  530.4 74.4 %all-gather.5.cloned.1.call-done = f32[24576,128]{1,0:T(8,128)} async-done(((f32[192,128]{1,0:T(8,128)}), f32[24576,128]{1,0:T(8,128)}) %all-gather.5.cloned.1.call-update) | async-done | bytes 12582928 | tf_op jit(solution)/shard_map/all_gather | solution.py:55
  604.8 2.2 multiply_reduce_fusion
  607.0 0.0 copy-done.5
  607.0 0.6 reshape_subtract_fusion
  607.6 59.2 %conditional.3 = (f32[1536,1536]{1,0:T(8,128)}) conditional(s32[]{:T(128)} %convert_element_type.4, (f32[1536,128]{1,0:T(8,128)S(1)}, f32[1536,128]{1,0:T(8,128)S(1)}, f32[1536,128]{1,0:T(8,128)S(1)}, f32[1536,128]{1,0:T(8,128)S(1)}, f32[1536,1536]{1,0:T(8,128)}) %tuple.24, (f32[1536,1536]{1,0:T(8,128)}, f32[1536,128]{1,0:T(8,128)S(1)}, ...), branch_computations={%region_4.5_spmd, %region_5.6_spmd} | conditional | flops 14539556864 | bytes 163596320 | solution.py:74
  607.8 8.5 %fusion.24 = f32[1536,1536]{1,0:T(8,128)} fusion(f32[1536,1536]{1,0:T(8,128)} %get-tuple-element.51), kind=kLoop, calls=%fused_computation.38 | loop fusion | flops 4718592 | bytes 18874368 | tf_op jit(solution)/shard_map/cond/branch_1_fun/jit(triu)/select_n | solution.py:14
  616.3 9.7 %copy.12 = f32[1536,1536]{0,1:T(8,128)} copy(f32[1536,1536]{1,0:T(8,128)} %fusion.24) | data formatting | bytes 18874368 | tf_op jit(solution)/shard_map/cond/branch_1_fun/jit(triu)/select_n | solution.py:14
  626.0 9.6 %copy.10 = f32[1536,1536]{0,1:T(8,128)} copy(f32[1536,1536]{1,0:T(8,128)} %get-tuple-element.51) | data formatting | bytes 18874368 | tf_op jit(solution)/shard_map
  635.6 0.0 copy-start.3
  635.6 15.4 %fusion.22 = f32[1536,1536]{1,0:T(8,128)} fusion(f32[1536,1536]{0,1:T(8,128)} %copy.10, f32[1536,1536]{1,0:T(8,128)} %get-tuple-element.51, s32[1536]{0:T(1024)S(1)} %iota_add_fusion.1, f32[1536,128]{1,0:T(8,128)S(1)} %get-tuple-element.53, f32[1536,128]{1,0:T(8,128)S(1)} %get-tuple-element.52), kind=kOutput, calls=%fused_computation.31 | convolution fusion | flops 7265058816 | bytes 29890560 | tf_op jit(solution)/shard_map/cond/branch_1_fun/dot_general | solution.py:8
  651.0 0.0 copy-done.3
  651.0 15.8 %fusion.25 = f32[1536,1536]{1,0:T(8,128)} fusion(f32[1536,1536]{1,0:T(8,128)} %fusion.22, f32[1536,1536]{0,1:T(8,128)S(1)} %copy-done.3, f32[1536]{0:T(1024)S(1)} %get-tuple-element.54, f32[1536,128]{1,0:T(8,128)S(1)} %get-tuple-element.56, f32[1536,128]{1,0:T(8,128)S(1)} %get-tuple-element.55, f32[1536,1536]{1,0:T(8,128)} %get-tuple-element.51), kind=kOutput, calls=%fused_computation.39 | convolution fusion | flops 7269777408 | bytes 39327744 | tf_op jit(solution)/shard_map/cond/branch_1_fun/dot_general | solution.py:8
  666.8 0.0 copy-start.1
  666.8 0.8 copy-done.1
  (3 shorter events, 0.0 us)
Async XLA Ops:
  7.2 385.0 %copy-start = (f32[128,128]{1,0:T(8,128)S(1)}, f32[128,128]{1,0:T(8,128)}, u32[]{:S(2)}) copy-start(f32[128,128]{1,0:T(8,128)} %param.11) | copy-start | bytes 196612
  7.2 79.7 %all-gather.3.cloned.1.call-start = ((), (), s32[]{:S(2)}) async-start(), calls=%async_computation.1 | async-start | bytes 12681216 | tf_op jit(solution)/shard_map/all_gather | solution.py:35
  7.9 382.2 %reduce-scatter.2.cloned.1.call-start = ((), (), s32[]{:S(2)}) async-start(), calls=%async_computation.2 | async-start | bytes 12681216 | tf_op jit(solution)/shard_map/reduce_scatter | solution.py:51
  115.2 12.7 %copy-start.2 = (f32[1536,1536]{0,1:T(8,128)S(1)}, f32[1536,1536]{0,1:T(8,128)}, u32[]{:S(2)}) copy-start(f32[1536,1536]{0,1:T(8,128)} %copy.13) | copy-start | bytes 28311556 | tf_op jit(solution)/shard_map/cond
  168.1 222.0 %copy-start.4 = (f32[192,128]{1,0:T(8,128)S(1)}, f32[192,128]{1,0:T(8,128)}, u32[]{:S(2)}) copy-start(f32[192,128]{1,0:T(8,128)} %param.10) | copy-start | bytes 294916
  170.1 436.8 %copy-start.5 = (f32[1,1536]{1,0:T(1,128)S(1)}, f32[1,1536]{1,0:T(1,128)}, u32[]{:S(2)}) copy-start(f32[1,1536]{1,0:T(1,128)} %param.9) | copy-start | bytes 18436
  170.2 358.0 %all-reduce.2.cloned.1.call-start = ((), (), s32[]{:S(2)}) async-start(), calls=%async_computation.3 | async-start | bytes 131072 | tf_op jit(solution)/shard_map/psum | solution.py:52
  392.1 212.7 %all-gather.5.cloned.1.call-start = ((), (), s32[]{:S(2)}) async-start(), calls=%async_computation.4 | async-start | bytes 12681216 | tf_op jit(solution)/shard_map/all_gather | solution.py:55
  635.6 15.4 %copy-start.3 = (f32[1536,1536]{0,1:T(8,128)S(1)}, f32[1536,1536]{0,1:T(8,128)}, u32[]{:S(2)}) copy-start(f32[1536,1536]{0,1:T(8,128)} %copy.12) | copy-start | bytes 28311556 | tf_op jit(solution)/shard_map/cond
  666.8 0.8 copy-start.1
Sparse Core Ops, SparseCore 0:
  11.1 75.7 all-gather.2
  170.3 219.7 reduce-scatter.1
  395.4 132.6 all-reduce.1
  532.1 72.5 all-gather.4
where the time goes:
time: 679 us; the launch traced here: 674 us
  waiting for transfers between devices  508 us (75%)
  matrix products  67.9 us (10%)
  local copies, waits for them, and re-layouts  53.7 us (8%)
  other arithmetic  21 us (3%)
  between operations  14.1 us (2%)
  loops' own time  9.41 us (1%)
    reduce_scatter x1, waiting for transfers between devices, body(): lax.psum_scatter(partial_value, ('row', 'col'), scatter_dimension=0, tile...  220 us
    psum x1, waiting for transfers between devices, body(): gram_sum = lax.psum(product(vectors.T, z_piece), ('row', 'col'))  135 us
    all_gather x1, waiting for transfers between devices, body(): v_whole = lax.all_gather(vectors, ('row', 'col'), axis=0, tiled=True)  78.2 us
    all_gather x1, waiting for transfers between devices, body(): w_whole = lax.all_gather(w_piece, ('row', 'col'), axis=0, tiled=True)  74.4 us
    dot_general x9, matrix products, product(): jnp.dot(left, right, preferred_element_type=jnp.float32, precision=lax.Pr...  67.9 us
    select_n x2, local copies, waits for them, and re-layouts, sym_pair(): upper_part = jnp.triu(block, 1)  19.3 us
    another operation x2, local copies, waits for them, and re-layouts  19.2 us
    select_n x2, other arithmetic, sym_pair(): upper_part = jnp.triu(block, 1)  15.4 us
  transfers between devices with their start and end apart: 4, of which 4 were waited for; matrix products, arithmetic and copies ran while one was open for 0% of the time, Pallas kernels for 0%

commit v1 on v0

v1 whole, which is shorter than its diff:
```python
import functools

import jax
import jax.numpy as jnp
from jax import lax
from jax.experimental import pallas as pl
from jax.experimental.pallas import tpu as pltpu
from jax.sharding import PartitionSpec as P

TILE = 1536
NB = 128
GRID = 16
HALF = 8
ROWS = 8
COLS = 16
VPIECE = 192
ZPIECE = 96
MESH = pl.DeviceIdType.MESH
F32 = jnp.float32
BF16 = jnp.bfloat16


def dot(left, right):
    return lax.dot_general(left, right, (((1,), (0,)), ((), ())), preferred_element_type=F32)


def dot_exact(left, right, dims=((1,), (0,))):
    return lax.dot_general(
        left, right, (dims, ((), ())), preferred_element_type=F32, precision=lax.Precision.HIGHEST
    )


def halves(value):
    high = value.astype(BF16)
    low = (value - high.astype(F32)).astype(BF16)
    return high, low


def member(tile, m):
    far = GRID - 1 - tile
    near_row = jnp.where(m <= tile, tile, jnp.where(m < HALF, m, m - HALF))
    near_col = jnp.where(m <= tile, m, jnp.where(m < HALF, tile, m - HALF + tile + 1))
    near_slot = jnp.where(m <= tile, 0, 1)
    far_row = jnp.where(m >= far, far, m)
    far_col = jnp.where(m >= far, m, GRID - far + m)
    far_slot = jnp.where(m > far, 0, 1)
    near = tile < HALF
    return (
        jnp.where(near, near_row, far_row),
        jnp.where(near, near_col, far_col),
        jnp.where(near, near_slot, far_slot),
    )


def put(src, dst, send_sem, recv_sem, to_row, to_col, row, col):
    here = jnp.logical_and(to_row == row, to_col == col)

    @pl.when(here)
    def _():
        pltpu.make_async_copy(src, dst, recv_sem).start()

    @pl.when(jnp.logical_not(here))
    def _():
        pltpu.make_async_remote_copy(
            src_ref=src, dst_ref=dst, send_sem=send_sem, recv_sem=recv_sem,
            device_id=(to_row, to_col), device_id_type=MESH,
        ).start()


def sent(src, send_sem, to_row, to_col, row, col):
    here = jnp.logical_and(to_row == row, to_col == col)

    @pl.when(jnp.logical_not(here))
    def _():
        pltpu.make_async_remote_copy(
            src_ref=src, dst_ref=src, send_sem=send_sem, recv_sem=send_sem,
            device_id=(to_row, to_col), device_id_type=MESH,
        ).wait_send()


def arrived(ref, sem):
    pltpu.make_async_copy(ref, ref, sem).wait()


def exchange(
    mat, lowd, vec, fac, xl_out, xrt_out, xl1_out, xrt0_out, d_out,
    abuf, ahi, alo, sym, vbuf, vcat, vtc, z, parts, zsum, zf, vd,
    gpart, g1, g1s, g2, g2s, gf, dmine, xl, xrt, xl1, xrt0,
    a_sem, v_send, v_recv, vd_send, vd_recv, r_send, r_recv, g_send, g_recv,
    z_send, z_recv, d_send, d_recv, o_sem,
):
    row = lax.axis_index("row")
    col = lax.axis_index("col")
    diag = row == col
    plain = row != col
    other = jnp.where(col < row, col, jnp.where(diag, GRID - 1 - row, col - row - 1))
    home = jnp.where(other < HALF, other, GRID - 1 - other)

    def part_copy(k):
        return pltpu.make_async_copy(
            mat.at[pl.ds(k * 384, 384)], abuf.at[pl.ds(k * 384, 384)], a_sem.at[k]
        )

    for k in range(4):
        part_copy(k).start()

    me = row * COLS + col
    bar = pltpu.get_barrier_semaphore()

    def greet(j, carry):
        to = lax.rem(me + j, ROWS * COLS)
        pl.semaphore_signal(
            bar, inc=1, device_id=(to // COLS, lax.rem(to, COLS)), device_id_type=MESH
        )
        return carry

    lax.fori_loop(1, ROWS * COLS, greet, 0)
    pl.semaphore_wait(bar, ROWS * COLS - 1)

    vtile = 2 * row + col // 8
    vpiece = lax.rem(col, 8)

    def v_args(j):
        m = lax.rem(j + 2 * vpiece, 16)
        return member(vtile, m)

    def v_put(j, carry):
        to_row, to_col, slot = v_args(j)
        put(vec, vbuf.at[slot, pl.ds(vpiece * VPIECE, VPIECE)], v_send.at[j], v_recv.at[slot],
            to_row, to_col, row, col)
        return carry

    lax.fori_loop(0, 16, v_put, 0)

    vfar = GRID - 1 - vtile

    @pl.when(vtile >= HALF)
    def _():
        for k in range(2):
            put(vec.at[pl.ds(k * ZPIECE, ZPIECE)], vd, vd_send.at[k], vd_recv,
                vfar, 2 * vpiece + k, row, col)

    for k in range(4):
        part_copy(k).wait()

        def split(s, carry):
            rows = pl.ds(pl.multiple_of(k * 384 + s * 32, 32), 32)
            high, low = halves(abuf[rows, :])
            ahi[rows, :] = high
            alo[rows, :] = low
            return carry

        lax.fori_loop(0, 12, split, 0)

    @pl.when(diag)
    def _():
        rr = lax.broadcasted_iota(jnp.int32, (256, 256), 0)
        cc = lax.broadcasted_iota(jnp.int32, (256, 256), 1)
        for p in range(6):
            at = slice(p * 256, p * 256 + 256)
            block = abuf[at, at]
            lower = jnp.where(rr > cc, block, 0.0)
            upper = jnp.where(rr < cc, block, 0.0)
            onto = jnp.where(rr == cc, block, 0.0)
            far_onto = jnp.where(rr == cc, jnp.broadcast_to(lowd[:, at], (256, 256)), 0.0)
            for s, full in ((0, lower + lower.T + onto), (1, upper + upper.T + far_onto)):
                high, low = halves(full)
                sym[s, 0, p] = high
                sym[s, 1, p] = low

    def cat_v(s):
        for p in range(6):
            at = slice(p * 256, p * 256 + 256)
            high, low = halves(vbuf[s, at, :])
            vcat[s, at, 0:128] = high
            vcat[s, at, 128:256] = low

    def cat_vt(s):
        for p in range(6):
            at = slice(p * 256, p * 256 + 256)
            high, low = halves(vbuf[s, at, :].T)
            vtc[s, 0:128, at] = high
            vtc[s, 128:256, at] = low

    def times(high, low, v):
        full = dot(high, v)
        return full[:, 0:128] + full[:, 128:256] + dot(low, v[:, 0:128])

    def times_t(vt, high, low):
        full = dot(vt, high)
        return full[0:128] + full[128:256] + dot(vt[0:128], low)

    def z_args(s, c):
        slot_m = jnp.where(col < row, row, jnp.where(
            diag, col, jnp.where(other < HALF, HALF + row, row)))
        if s == 0:
            to_row = row
            half = jnp.where(col <= row, 0, 1)
            m = col
        else:
            to_row = home
            half = jnp.where(other < HALF, 0, 1)
            m = slot_m
        return to_row, half * 16 + m

    def z_put(s, c):
        to_row, at = z_args(s, c)
        put(z.at[s, pl.ds(c * ZPIECE, ZPIECE)], parts.at[at], r_send.at[s, c], r_recv,
            to_row, c, row, col)

    def z_put_range(s, first, count):
        def one(j, carry):
            z_put(s, first + lax.rem(j + col, count))
            return carry

        lax.fori_loop(0, count, one, 0)

    def gram(s):
        high, low = halves(z[s])
        full = dot(vtc[s], high)
        return full[0:128] + full[128:256] + dot(vtc[s, 0:128, :], low)

    def g_start():
        def one(j, carry):
            c = lax.rem(j + col, COLS)
            put(gpart.at[pl.ds(pl.multiple_of(c * 8, 8), 8)], g1.at[col], g_send.at[0, c],
                g_recv.at[0], row, c, row, col)
            return carry

        lax.fori_loop(0, COLS, one, 0)

    arrived(vbuf.at[1], v_recv.at[1])
    cat_v(1)

    @pl.when(plain)
    def _():
        def panel(k, carry):
            rows = pl.ds(pl.multiple_of(k * 384, 384), 384)
            z[0, rows, :] = times(ahi[rows, :], alo[rows, :], vcat[1])
            z_put_range(0, k * 4, 4)
            return carry

        lax.fori_loop(0, 4, panel, 0)

    arrived(vbuf.at[0], v_recv.at[0])
    cat_vt(0)

    @pl.when(plain)
    def _():
        y = gram(0)
        gpart[...] = y + y.T
        g_start()

        def panel(k, carry):
            at = pl.ds(pl.multiple_of(k * 768, 768), 768)
            part = times_t(vtc[0], ahi[:, at], alo[:, at])
            z[1, at, :] = part.T
            z_put_range(1, k * 8, 8)
            return carry

        lax.fori_loop(0, 2, panel, 0)

    @pl.when(diag)
    def _():
        cat_v(0)
        cat_vt(1)
        for p in range(6):
            lo, hi = p * 256, p * 256 + 256
            at = slice(lo, hi)
            z0 = times(sym[0, 0, p], sym[0, 1, p], vcat[0, at, :])
            z1 = times(sym[1, 0, p], sym[1, 1, p], vcat[1, at, :])
            if p > 0:
                z0 += times(ahi[at, 0:lo], alo[at, 0:lo], vcat[0, 0:lo, :])
                z1 += times_t(vtc[1, :, 0:lo], ahi[0:lo, at], alo[0:lo, at]).T
            if p < 5:
                z1 += times(ahi[at, hi:], alo[at, hi:], vcat[1, hi:, :])
                z0 += times_t(vtc[0, :, hi:], ahi[hi:, at], alo[hi:, at]).T
            z[0, at, :] = z0
            z[1, at, :] = z1
        z_put_range(0, 0, 16)
        z_put_range(1, 0, 16)
        gpart[...] = gram(0) + gram(1)
        g_start()

    arrived(g1, g_recv.at[0])
    g1s[...] = jnp.sum(g1[...], axis=0)

    def g_line(j, carry):
        r = lax.rem(j + row, ROWS)
        put(g1s, g2.at[row], g_send.at[1, r], g_recv.at[1], r, col, row, col)
        return carry

    lax.fori_loop(0, ROWS, g_line, 0)
    arrived(g2, g_recv.at[1])
    g2s[...] = jnp.sum(g2[...], axis=0)

    def g_row(j, carry):
        c = lax.rem(j + col, COLS)
        put(g2s, gf.at[pl.ds(pl.multiple_of(col * 8, 8), 8)], g_send.at[2, c], g_recv.at[2],
            row, c, row, col)
        return carry

    lax.fori_loop(0, COLS, g_row, 0)

    arrived(parts, r_recv)
    zsum[0] = jnp.sum(parts[0:16], axis=0)
    zsum[1] = jnp.sum(parts[16:32], axis=0)

    def zf_args(j, half):
        tile = row if half == 0 else GRID - 1 - row
        return member(tile, lax.rem(j + col, 16))

    def zf_put(j, carry):
        for half in range(2):
            to_row, to_col, slot = zf_args(j, half)
            put(zsum.at[half], zf.at[slot, pl.ds(col * ZPIECE, ZPIECE)], z_send.at[half, j],
                z_recv.at[slot], to_row, to_col, row, col)
        return carry

    lax.fori_loop(0, 16, zf_put, 0)

    arrived(gf, g_recv.at[2])
    fac_value = fac[...]
    middle = dot_exact(dot_exact(fac_value, gf[...], ((0,), (0,))), fac_value)

    arrived(vd, vd_recv)
    v_far = vd[...]
    w_far = dot_exact(zsum[1], fac_value) - 0.5 * dot_exact(v_far, middle)
    sums = dot_exact(jnp.ones((8, 128), F32), v_far * w_far, ((1,), (1,)))
    dmine[...] = jnp.concatenate([sums, jnp.zeros((8, 32), F32)], axis=1)

    def d_put(j, carry):
        c = lax.rem(j + col, COLS)
        put(dmine, d_out.at[col], d_send.at[c], d_recv, row, c, row, col)
        return carry

    lax.fori_loop(0, COLS, d_put, 0)

    both = jnp.concatenate([fac_value, -0.5 * middle], axis=0)
    both_high, both_low = halves(both)
    both_t = both.T
    both_t_high, both_t_low = halves(both_t)

    def w_plain(s, out):
        def panel(k, carry):
            rows = pl.ds(pl.multiple_of(k * 256, 256), 256)
            v_high, v_low = halves(vbuf[s, rows, :])
            z_high, z_low = halves(zf[s, rows, :])
            high = jnp.concatenate([z_high, v_high], axis=1)
            low = jnp.concatenate([z_low, v_low], axis=1)
            w = dot(high, both_high) + dot(high, both_low) + dot(low, both_high)
            w_high, w_low = halves(w)
            out[rows, :] = jnp.concatenate([v_high, w_high, v_low, w_low], axis=1)
            return carry

        lax.fori_loop(0, 6, panel, 0)

    def w_turned(s, out):
        def panel(k, carry):
            rows = pl.ds(pl.multiple_of(k * 256, 256), 256)
            v_high, v_low = halves(vbuf[s, rows, :].T)
            z_high, z_low = halves(zf[s, rows, :].T)
            high = jnp.concatenate([z_high, v_high], axis=0)
            low = jnp.concatenate([z_low, v_low], axis=0)
            w = dot(both_t_high, high) + dot(both_t_low, high) + dot(both_t_high, low)
            w_high, w_low = halves(w)
            out[:, rows] = jnp.concatenate([w_high, v_high, w_low, v_low], axis=0)
            return carry

        lax.fori_loop(0, 6, panel, 0)

    arrived(zf.at[1], z_recv.at[1])
    w_turned(1, xrt)
    pltpu.make_async_copy(xrt, xrt_out, o_sem.at[0]).start()
    arrived(zf.at[0], z_recv.at[0])
    w_plain(0, xl)
    pltpu.make_async_copy(xl, xl_out, o_sem.at[1]).start()

    @pl.when(diag)
    def _():
        w_plain(1, xl1)
        w_turned(0, xrt0)
        pltpu.make_async_copy(xl1, xl1_out, o_sem.at[2]).start()
        pltpu.make_async_copy(xrt0, xrt0_out, o_sem.at[3]).start()

    arrived(d_out, d_recv)

    def all_sent(j, carry):
        to_row, to_col, slot = v_args(j)
        sent(vec, v_send.at[j], to_row, to_col, row, col)
        for s in range(2):
            to_row, at = z_args(s, j)
            sent(z.at[s, pl.ds(0, ZPIECE)], r_send.at[s, j], to_row, j, row, col)
            to_row, to_col, slot = zf_args(j, s)
            sent(zsum.at[s], z_send.at[s, j], to_row, to_col, row, col)
        sent(g1s, g_send.at[0, j], row, j, row, col)
        sent(g2s, g_send.at[2, j], row, j, row, col)
        sent(dmine, d_send.at[j], row, j, row, col)
        return carry

    lax.fori_loop(0, 16, all_sent, 0)

    def line_sent(j, carry):
        sent(g1s, g_send.at[1, j], j, col, row, col)
        return carry

    lax.fori_loop(0, ROWS, line_sent, 0)

    @pl.when(vtile >= HALF)
    def _():
        for k in range(2):
            sent(vd, vd_send.at[k], vfar, 2 * vpiece + k, row, col)

    arrived(xrt, o_sem.at[0])
    arrived(xl, o_sem.at[1])

    @pl.when(diag)
    def _():
        arrived(xl1, o_sem.at[2])
        arrived(xrt0, o_sem.at[3])


def update(mat, xl, xrt, d, fard, xl1_hbm, xrt0_hbm, out, far_out, xl1, xrt0, sem):
    step = pl.program_id(0)
    diag = lax.axis_index("row") == lax.axis_index("col")

    @pl.when(jnp.logical_and(diag, step == 0))
    def _():
        first = pltpu.make_async_copy(xl1_hbm, xl1, sem.at[0])
        second = pltpu.make_async_copy(xrt0_hbm, xrt0, sem.at[1])
        first.start()
        second.start()
        first.wait()
        second.wait()

    @pl.when(step == 0)
    def _():
        lane = lax.broadcasted_iota(jnp.int32, (128, TILE), 1)
        start = jnp.zeros((128, TILE), jnp.int32)
        for k in range(1, 16):
            start += jnp.where(lane >= k * ZPIECE, ZPIECE, 0)
        pick = jnp.where(lane - start == lax.broadcasted_iota(jnp.int32, (128, TILE), 0), 1.0, 0.0)
        spread = dot_exact(d[:, 0, :], pick)
        piece = lax.broadcasted_iota(jnp.int32, (16, TILE), 0) * ZPIECE
        whole = jnp.sum(jnp.where(piece == start[0:16], spread, 0.0), axis=0, keepdims=True)
        far_out[...] = fard[...] - 2.0 * whole

    def change(left, right):
        high, low = left[:, 0:256], left[:, 256:512]
        return dot(high, right[0:256]) + dot(high, right[256:512]) + dot(low, right[0:256])

    rows = pl.ds(pl.multiple_of(step * 256, 256), 256)

    @pl.when(jnp.logical_not(diag))
    def _():
        out[...] = mat[...] - change(xl[rows, :], xrt[...])

    @pl.when(diag)
    def _():
        lead = change(xl[rows, :], xrt0[...])
        far = change(xl1[rows, :], xrt[...])
        at_row = lax.broadcasted_iota(jnp.int32, (256, TILE), 0) + step * 256
        at_col = lax.broadcasted_iota(jnp.int32, (256, TILE), 1)
        out[...] = mat[...] - jnp.where(at_row >= at_col, lead, far)


def body(matrix, far_diag, vectors, factors):
    any_spec = pl.BlockSpec(memory_space=pl.ANY)
    vmem_spec = pl.BlockSpec(memory_space=pltpu.VMEM)
    dma = pltpu.SemaphoreType.DMA
    xl_shape = jax.ShapeDtypeStruct((TILE, 512), BF16)
    xrt_shape = jax.ShapeDtypeStruct((512, TILE), BF16)
    xl, xrt, xl1, xrt0, d = pl.pallas_call(
        exchange,
        name="exchange",
        out_shape=(xl_shape, xrt_shape, xl_shape, xrt_shape,
                   jax.ShapeDtypeStruct((16, 8, 128), F32)),
        in_specs=[any_spec, vmem_spec, vmem_spec, vmem_spec],
        out_specs=(any_spec, any_spec, any_spec, any_spec, vmem_spec),
        scratch_shapes=[
            pltpu.VMEM((TILE, TILE), F32),
            pltpu.VMEM((TILE, TILE), BF16),
            pltpu.VMEM((TILE, TILE), BF16),
            pltpu.VMEM((2, 2, 6, 256, 256), BF16),
            pltpu.VMEM((2, TILE, NB), F32),
            pltpu.VMEM((2, TILE, 2 * NB), BF16),
            pltpu.VMEM((2, 2 * NB, TILE), BF16),
            pltpu.VMEM((2, TILE, NB), F32),
            pltpu.VMEM((32, ZPIECE, NB), F32),
            pltpu.VMEM((2, ZPIECE, NB), F32),
            pltpu.VMEM((2, TILE, NB), F32),
            pltpu.VMEM((ZPIECE, NB), F32),
            pltpu.VMEM((NB, NB), F32),
            pltpu.VMEM((16, 8, NB), F32),
            pltpu.VMEM((8, NB), F32),
            pltpu.VMEM((8, 8, NB), F32),
            pltpu.VMEM((8, NB), F32),
            pltpu.VMEM((NB, NB), F32),
            pltpu.VMEM((8, NB), F32),
            pltpu.VMEM((TILE, 512), BF16),
            pltpu.VMEM((512, TILE), BF16),
            pltpu.VMEM((TILE, 512), BF16),
            pltpu.VMEM((512, TILE), BF16),
            dma((4,)),
            dma((16,)),
            dma((2,)),
            dma((2,)),
            dma,
            dma((2, 16)),
            dma,
            dma((3, 16)),
            dma((3,)),
            dma((2, 16)),
            dma((2,)),
            dma((16,)),
            dma,
            dma((4,)),
        ],
        compiler_params=pltpu.CompilerParams(
            collective_id=0, has_side_effects=True, vmem_limit_bytes=56 * 2**20
        ),
    )(matrix, far_diag, vectors, factors)
    whole = lambda *shape: pl.BlockSpec(shape, lambda i: (0,) * len(shape))
    updated, far_updated = pl.pallas_call(
        update,
        name="update",
        grid=(6,),
        out_shape=(jax.ShapeDtypeStruct((TILE, TILE), F32), jax.ShapeDtypeStruct((1, TILE), F32)),
        in_specs=[
            pl.BlockSpec((256, TILE), lambda i: (i, 0)),
            whole(TILE, 512),
            whole(512, TILE),
            whole(16, 8, 128),
            whole(1, TILE),
            any_spec,
            any_spec,
        ],
        out_specs=(pl.BlockSpec((256, TILE), lambda i: (i, 0)), whole(1, TILE)),
        scratch_shapes=[
            pltpu.VMEM((TILE, 512), BF16),
            pltpu.VMEM((512, TILE), BF16),
            dma((2,)),
        ],
        compiler_params=pltpu.CompilerParams(vmem_limit_bytes=48 * 2**20),
    )(matrix, xl, xrt, d, far_diag, xl1, xrt0)
    return updated, far_updated


def solution(mesh):
    in_specs = (P("row", "col"), P("row", None), P(("row", "col"), None), P())
    out_specs = (P("row", "col"), P("row", None))
    return jax.shard_map(body, mesh=mesh, in_specs=in_specs, out_specs=out_specs, check_vma=False)
```

time: 679 us -> 145 us (0.21)
  waiting for transfers between devices: 508 us -> 0 us
  Pallas kernels: 0 us -> 139 us
  matrix products: 67.9 us -> 0 us
  local copies, waits for them, and re-layouts: 53.7 us -> 5.06 us
  other arithmetic: 21 us -> 0 us
  between operations: 14.1 us -> 0.83 us
  loops' own time: 9.41 us -> 0 us
    reduce_scatter x1 -> x0, waiting for transfers between devices: 220 us -> none  [body(): lax.psum_scatter(partial_value, ('row', 'col'), scatter_dimension=0, tile...]
    all_gather x2 -> x0, waiting for transfers between devices: 153 us -> none  [the longest x1 78.2 us: body(): v_whole = lax.all_gather(vectors, ('row', 'col'), axis=0, tiled=True)]
    pallas_call x0 -> x2, Pallas kernels: none -> 139 us  [the longest x1 124 us: body(): pl.pallas_call(exchange, name='exchange', out_shape=(xl_shape, xrt_shape,...]
    psum x1 -> x0, waiting for transfers between devices: 135 us -> none  [body(): gram_sum = lax.psum(product(vectors.T, z_piece), ('row', 'col'))]
    dot_general x9 -> x0, matrix products: 67.9 us -> none  [product(): jnp.dot(left, right, preferred_element_type=jnp.float32, precision=lax.Pr...]
    select_n x2 -> x0, local copies, waits for them, and re-layouts: 19.3 us -> none  [sym_pair(): upper_part = jnp.triu(block, 1)]
    another operation x2 -> x0, local copies, waits for them, and re-layouts: 19.2 us -> none
    select_n x2 -> x0, other arithmetic: 15.4 us -> none  [sym_pair(): upper_part = jnp.triu(block, 1)]
  transfers between devices with their start and end apart: 4 -> 0, of which waited for: 4 -> 0; matrix products, arithmetic and copies ran while one was open for 0% -> 0% of each run, Pallas kernels for 0% -> 0%
where the time goes in v1:
time: 145 us
  Pallas kernels  139 us (96%)
  local copies, waits for them, and re-layouts  5.06 us (3%)
    pallas_call x1, Pallas kernels, body(): pl.pallas_call(exchange, name='exchange', out_shape=(xl_shape, xrt_shape,...  124 us
    pallas_call x1, Pallas kernels, body(): pl.pallas_call(update, name='update', grid=(6,), out_shape=(jax.ShapeDtyp...  14.6 us
    unnamed x10, local copies, waits for them, and re-layouts  5.06 us

profile of v1, /device:TPU:0, one launch (start us, length us, event | category | flops | bytes accessed | tf_op | source)
XLA Modules:
  0.0 144.9 jit_solution(10223602611389569099)
XLA Ops:
  0.6 0.0 copy-start.4
  0.6 124.5 %exchange.1 = (bf16[1536,512]{1,0:T(8,128)(2,1)}, bf16[512,1536]{1,0:T(8,128)(2,1)}, bf16[1536,512]{1,0:T(8,128)(2,1)}, bf16[512,1536]{1,0:T(8,128)(2,1)}, f32[16,8,128]{2,1,0:T(8,128)}) custom-call(f32[1536,1536]{1,0:T(8,128)} %mat.3, f32[1,1536]{1,0:T(1,128)} %fard.1, f32[192,128]{1,0:T(8,128)} %vec.1, f32[128,128]{1,0:T(8,128)} %fac.1), custom_call_target="tpu_custom_call" | custom-call | tf_op jit(solution)/shard_map/exchange/pallas_call | solution.py:473
  125.1 0.0 copy-done.4
  125.1 0.0 copy-start
  125.1 1.4 copy-done
  126.5 0.0 copy-start.1
  126.5 1.4 copy-done.1
  127.9 0.0 copy-start.2
  128.0 1.4 copy-done.2
  129.4 0.0 copy-start.3
  129.4 0.8 copy-done.3
  130.2 14.6 %update.1 = (f32[1536,1536]{1,0:T(8,128)}, f32[1,1536]{1,0:T(1,128)}) custom-call(f32[1536,1536]{1,0:T(8,128)} %mat.3, bf16[1536,512]{1,0:T(8,128)(2,1)S(1)} %copy-done, bf16[512,1536]{1,0:T(8,128)(2,1)S(1)} %copy-done.1, f32[16,8,128]{2,1,0:T(8,128)S(1)} %copy-done.3, f32[1,1536]{1,0:T(1,128)S(1)} %copy-done.4, bf16[1536,512]{1,0:T(8,128)(2,1)S(1)} %copy-done.2, ...), custom_call_target="tpu_custom_call" | custom-call | tf_op jit(solution)/shard_map/update/pallas_call | solution.py:524
Async XLA Ops:
  0.6 124.5 %copy-start.4 = (f32[1,1536]{1,0:T(1,128)S(1)}, f32[1,1536]{1,0:T(1,128)}, u32[]{:S(2)}) copy-start(f32[1,1536]{1,0:T(1,128)} %fard.1) | copy-start | bytes 18436
  125.1 1.4 copy-start
  126.5 1.4 copy-start.1
  127.9 1.4 copy-start.2
  129.4 0.8 copy-start.3

commit v2 on v1

--- a/solution.py
+++ b/solution.py
@@ -12,6 +12,7 @@
 GRID = 16
 HALF = 8
 ROWS = 8
+LINE = ((0, 1), (1, 0), (3, 0), (1, 1), (3, 1), (2, 0), (2, 1))
 COLS = 16
 VPIECE = 192
 ZPIECE = 96
@@ -67,7 +68,7 @@
         ).start()
 
 
-def sent(src, send_sem, to_row, to_col, row, col):
+def sent(src, dst, send_sem, recv_sem, to_row, to_col, row, col):
     here = jnp.logical_and(to_row == row, to_col == col)
 
     @pl.when(jnp.logical_not(here))
@@ -84,17 +85,21 @@
 
 def exchange(
     mat, lowd, vec, fac, xl_out, xrt_out, xl1_out, xrt0_out, d_out,
-    abuf, ahi, alo, sym, vbuf, vcat, vtc, z, parts, zsum, zf, vd,
+    abuf, ahi, alo, sym, vline, vbuf, vcat, vtc, z, parts, lpart, lsend, zsum, zf, vd,
     gpart, g1, g1s, g2, g2s, gf, dmine, xl, xrt, xl1, xrt0,
-    a_sem, v_send, v_recv, vd_send, vd_recv, r_send, r_recv, g_send, g_recv,
-    z_send, z_recv, d_send, d_recv, o_sem,
+    a_sem, vl_send, vl_recv, vf_send, vo_send, v_recv, vd_send, vd_recv, r_send, r_recv,
+    l_send, l_recv, g_send, g_recv, z_send, z_recv, d_send, d_recv, o_sem,
 ):
     row = lax.axis_index("row")
     col = lax.axis_index("col")
     diag = row == col
     plain = row != col
     other = jnp.where(col < row, col, jnp.where(diag, GRID - 1 - row, col - row - 1))
-    home = jnp.where(other < HALF, other, GRID - 1 - other)
+    far = GRID - 1 - row
+    x, core = row // 2, lax.rem(row, 2)
+
+    def line_row(step):
+        return lax.rem(x + step[0], 4) * 2 + lax.rem(core + step[1], 2)
 
     def part_copy(k):
         return pltpu.make_async_copy(
@@ -104,43 +109,22 @@
     for k in range(4):
         part_copy(k).start()
 
-    me = row * COLS + col
     bar = pltpu.get_barrier_semaphore()
 
     def greet(j, carry):
-        to = lax.rem(me + j, ROWS * COLS)
         pl.semaphore_signal(
-            bar, inc=1, device_id=(to // COLS, lax.rem(to, COLS)), device_id_type=MESH
+            bar, inc=1, device_id=(row, lax.rem(col + j, COLS)), device_id_type=MESH
         )
         return carry
 
-    lax.fori_loop(1, ROWS * COLS, greet, 0)
-    pl.semaphore_wait(bar, ROWS * COLS - 1)
-
-    vtile = 2 * row + col // 8
-    vpiece = lax.rem(col, 8)
-
-    def v_args(j):
-        m = lax.rem(j + 2 * vpiece, 16)
-        return member(vtile, m)
-
-    def v_put(j, carry):
-        to_row, to_col, slot = v_args(j)
-        put(vec, vbuf.at[slot, pl.ds(vpiece * VPIECE, VPIECE)], v_send.at[j], v_recv.at[slot],
-            to_row, to_col, row, col)
-        return carry
-
-    lax.fori_loop(0, 16, v_put, 0)
-
-    vfar = GRID - 1 - vtile
-
-    @pl.when(vtile >= HALF)
-    def _():
-        for k in range(2):
-            put(vec.at[pl.ds(k * ZPIECE, ZPIECE)], vd, vd_send.at[k], vd_recv,
-                vfar, 2 * vpiece + k, row, col)
-
-    for k in range(4):
+    lax.fori_loop(1, COLS, greet, 0)
+    for step in LINE:
+        pl.semaphore_signal(bar, inc=1, device_id=(line_row(step), col), device_id_type=MESH)
+
+    own = pltpu.make_async_copy(vec, vline.at[row], vl_recv.at[row])
+    own.start()
+
+    def split_part(k):
         part_copy(k).wait()
 
         def split(s, carry):
@@ -151,6 +135,89 @@
             return carry
 
         lax.fori_loop(0, 12, split, 0)
+
+    split_part(0)
+    split_part(1)
+    pl.semaphore_wait(bar, COLS - 1 + ROWS - 1)
+
+    vtile = 2 * row + col // 8
+    vpiece = lax.rem(col, 8)
+    parity = col // 8
+    vlead_row = jnp.where(vtile < HALF, vtile, GRID - 1 - vtile)
+
+    def v_line(j, to_row):
+        return pltpu.make_async_remote_copy(
+            src_ref=vec, dst_ref=vline.at[row], send_sem=vl_send.at[j],
+            recv_sem=vl_recv.at[row], device_id=(to_row, col), device_id_type=MESH,
+        )
+
+    def v_line_each(act):
+        @pl.when(vlead_row != row)
+        def _():
+            act(v_line(7, vlead_row))
+
+        for j, step in enumerate(LINE):
+            to_row = line_row(step)
+
+            @pl.when(jnp.logical_and(to_row != vlead_row, to_row <= GRID - 1 - vtile))
+            def _():
+                act(v_line(j, to_row))
+
+    v_line_each(lambda copy: copy.start())
+
+    lead_near = lax.rem(row, 2) == parity
+    lead_src = jnp.where(lead_near, row, far) // 2
+    v_rows = pl.ds(vpiece * VPIECE, VPIECE)
+
+    def v_lead_each(act):
+        def one(j, carry):
+            c = lax.rem(j + col, COLS)
+
+            @pl.when(jnp.logical_or(c == row, (c < row) == lead_near))
+            def _():
+                slot = jnp.where(jnp.logical_or(c != row, lead_near), 0, 1)
+                act(vline.at[lead_src], vbuf.at[slot, v_rows], vf_send.at[j], v_recv.at[slot],
+                    row, c, row, col)
+
+            return carry
+
+        lax.fori_loop(0, COLS, one, 0)
+
+        @pl.when(jnp.logical_not(lead_near))
+        def _():
+            for k in range(2):
+                act(vline.at[lead_src, pl.ds(k * ZPIECE, ZPIECE)], vd, vd_send.at[k], vd_recv,
+                    row, 2 * vpiece + k, row, col)
+
+    def v_other_each(act, before):
+        for j, step in enumerate(((0, 0),) + LINE):
+            src = line_row(step)
+            tile = 2 * src + parity
+
+            @pl.when(jnp.logical_and(tile <= far, src != lead_src))
+            def _():
+                before(src)
+
+            @pl.when(tile < row)
+            def _():
+                act(vline.at[src], vbuf.at[1, v_rows], vo_send.at[j, 0], v_recv.at[1],
+                    row, tile, row, col)
+
+            @pl.when(tile < far)
+            def _():
+                act(vline.at[src], vbuf.at[1, v_rows], vo_send.at[j, 1], v_recv.at[1],
+                    row, tile + row + 1, row, col)
+
+    arrived(vline.at[lead_src], vl_recv.at[lead_src])
+    v_lead_each(put)
+    v_other_each(put, lambda src: arrived(vline.at[src], vl_recv.at[src]))
+
+    @pl.when(jnp.logical_and(vtile > far, lead_src != row))
+    def _():
+        arrived(vline.at[row], vl_recv.at[row])
+
+    split_part(2)
+    split_part(3)
 
     @pl.when(diag)
     def _():
@@ -190,27 +257,13 @@
         full = dot(vt, high)
         return full[0:128] + full[128:256] + dot(vt[0:128], low)
 
-    def z_args(s, c):
-        slot_m = jnp.where(col < row, row, jnp.where(
-            diag, col, jnp.where(other < HALF, HALF + row, row)))
-        if s == 0:
-            to_row = row
-            half = jnp.where(col <= row, 0, 1)
-            m = col
-        else:
-            to_row = home
-            half = jnp.where(other < HALF, 0, 1)
-            m = slot_m
-        return to_row, half * 16 + m
-
-    def z_put(s, c):
-        to_row, at = z_args(s, c)
-        put(z.at[s, pl.ds(c * ZPIECE, ZPIECE)], parts.at[at], r_send.at[s, c], r_recv,
-            to_row, c, row, col)
-
-    def z_put_range(s, first, count):
+    def z_put_range(s, first, count, act=None):
+        act = act or put
+
         def one(j, carry):
-            z_put(s, first + lax.rem(j + col, count))
+            c = first + lax.rem(j + col, count)
+            act(z.at[s, pl.ds(c * ZPIECE, ZPIECE)], parts.at[s, col], r_send.at[s, c],
+                r_recv.at[s], row, c, row, col)
             return carry
 
         lax.fori_loop(0, count, one, 0)
@@ -229,28 +282,11 @@
 
         lax.fori_loop(0, COLS, one, 0)
 
-    arrived(vbuf.at[1], v_recv.at[1])
-    cat_v(1)
-
-    @pl.when(plain)
-    def _():
-        def panel(k, carry):
-            rows = pl.ds(pl.multiple_of(k * 384, 384), 384)
-            z[0, rows, :] = times(ahi[rows, :], alo[rows, :], vcat[1])
-            z_put_range(0, k * 4, 4)
-            return carry
-
-        lax.fori_loop(0, 4, panel, 0)
-
     arrived(vbuf.at[0], v_recv.at[0])
     cat_vt(0)
 
     @pl.when(plain)
     def _():
-        y = gram(0)
-        gpart[...] = y + y.T
-        g_start()
-
         def panel(k, carry):
             at = pl.ds(pl.multiple_of(k * 768, 768), 768)
             part = times_t(vtc[0], ahi[:, at], alo[:, at])
@@ -259,6 +295,22 @@
             return carry
 
         lax.fori_loop(0, 2, panel, 0)
+
+    arrived(vbuf.at[1], v_recv.at[1])
+    cat_v(1)
+
+    @pl.when(plain)
+    def _():
+        def panel(k, carry):
+            rows = pl.ds(pl.multiple_of(k * 384, 384), 384)
+            z[0, rows, :] = times(ahi[rows, :], alo[rows, :], vcat[1])
+            return carry
+
+        lax.fori_loop(0, 4, panel, 0)
+        y = gram(0)
+        gpart[...] = y + y.T
+        g_start()
+        z_put_range(0, 0, 16)
 
     @pl.when(diag)
     def _():
@@ -277,10 +329,10 @@
                 z0 += times_t(vtc[0, :, hi:], ahi[hi:, at], alo[hi:, at]).T
             z[0, at, :] = z0
             z[1, at, :] = z1
-        z_put_range(0, 0, 16)
         z_put_range(1, 0, 16)
         gpart[...] = gram(0) + gram(1)
         g_start()
+        z_put_range(0, 0, 16)
 
     arrived(g1, g_recv.at[0])
     g1s[...] = jnp.sum(g1[...], axis=0)
@@ -291,6 +343,36 @@
         return carry
 
     lax.fori_loop(0, ROWS, g_line, 0)
+
+    arrived(parts.at[1], r_recv.at[1])
+    for step in LINE:
+        to = line_row(step)
+
+        @pl.when(to < row)
+        def _():
+            lsend[to] = parts[1, to] + parts[1, to + row + 1]
+
+    def l_copy(src, to, k):
+        return pltpu.make_async_remote_copy(
+            src_ref=src, dst_ref=lpart.at[row, k], send_sem=l_send.at[to, k],
+            recv_sem=l_recv.at[row], device_id=(to, col), device_id_type=MESH,
+        )
+
+    def l_each(act):
+        for step in LINE:
+            to = line_row(step)
+
+            @pl.when(to < row)
+            def _():
+                act(l_copy(lsend.at[to], to, 0))
+
+            @pl.when(to > row)
+            def _():
+                act(l_copy(parts.at[1, to + row + 1], to, 0))
+                act(l_copy(parts.at[1, GRID - to + row], to, 1))
+
+    l_each(lambda copy: copy.start())
+
     arrived(g2, g_recv.at[1])
     g2s[...] = jnp.sum(g2[...], axis=0)
 
@@ -302,9 +384,28 @@
 
     lax.fori_loop(0, COLS, g_row, 0)
 
-    arrived(parts, r_recv)
-    zsum[0] = jnp.sum(parts[0:16], axis=0)
-    zsum[1] = jnp.sum(parts[16:32], axis=0)
+    arrived(parts.at[0], r_recv.at[0])
+    zsum[0] = parts[1, 2 * row + 1]
+    zsum[1] = parts[1, row]
+
+    def add_lead(c, carry):
+        zsum[jnp.where(c <= row, 0, 1)] += parts[0, c]
+        return carry
+
+    lax.fori_loop(0, COLS, add_lead, 0)
+    for step in LINE:
+        src = line_row(step)
+
+        @pl.when(src < row)
+        def _():
+            arrived(lpart.at[src], l_recv.at[src])
+            zsum[0] += lpart[src, 0]
+            zsum[1] += lpart[src, 1]
+
+        @pl.when(src > row)
+        def _():
+            arrived(lpart.at[src, 0], l_recv.at[src])
+            zsum[0] += lpart[src, 0]
 
     def zf_args(j, half):
         tile = row if half == 0 else GRID - 1 - row
@@ -385,31 +486,30 @@
 
     arrived(d_out, d_recv)
 
+    v_line_each(lambda copy: copy.wait_send())
+    v_lead_each(sent)
+    v_other_each(sent, lambda src: None)
+    z_put_range(0, 0, 16, sent)
+    z_put_range(1, 0, 16, sent)
+    l_each(lambda copy: copy.wait_send())
+
     def all_sent(j, carry):
-        to_row, to_col, slot = v_args(j)
-        sent(vec, v_send.at[j], to_row, to_col, row, col)
-        for s in range(2):
-            to_row, at = z_args(s, j)
-            sent(z.at[s, pl.ds(0, ZPIECE)], r_send.at[s, j], to_row, j, row, col)
-            to_row, to_col, slot = zf_args(j, s)
-            sent(zsum.at[s], z_send.at[s, j], to_row, to_col, row, col)
-        sent(g1s, g_send.at[0, j], row, j, row, col)
-        sent(g2s, g_send.at[2, j], row, j, row, col)
-        sent(dmine, d_send.at[j], row, j, row, col)
+        for half in range(2):
+            to_row, to_col, slot = zf_args(j, half)
+            sent(zsum.at[half], zsum.at[half], z_send.at[half, j], None,
+                 to_row, to_col, row, col)
+        sent(g1s, g1s, g_send.at[0, j], None, row, j, row, col)
+        sent(g2s, g2s, g_send.at[2, j], None, row, j, row, col)
+        sent(dmine, dmine, d_send.at[j], None, row, j, row, col)
         return carry
 
     lax.fori_loop(0, 16, all_sent, 0)
 
     def line_sent(j, carry):
-        sent(g1s, g_send.at[1, j], j, col, row, col)
+        sent(g1s, g1s, g_send.at[1, j], None, j, col, row, col)
         return carry
 
     lax.fori_loop(0, ROWS, line_sent, 0)
-
-    @pl.when(vtile >= HALF)
-    def _():
-        for k in range(2):
-            sent(vd, vd_send.at[k], vfar, 2 * vpiece + k, row, col)
 
     arrived(xrt, o_sem.at[0])
     arrived(xl, o_sem.at[1])
@@ -482,11 +582,14 @@
             pltpu.VMEM((TILE, TILE), BF16),
             pltpu.VMEM((TILE, TILE), BF16),
             pltpu.VMEM((2, 2, 6, 256, 256), BF16),
+            pltpu.VMEM((ROWS, VPIECE, NB), F32),
             pltpu.VMEM((2, TILE, NB), F32),
             pltpu.VMEM((2, TILE, 2 * NB), BF16),
             pltpu.VMEM((2, 2 * NB, TILE), BF16),
             pltpu.VMEM((2, TILE, NB), F32),
-            pltpu.VMEM((32, ZPIECE, NB), F32),
+            pltpu.VMEM((2, COLS, ZPIECE, NB), F32),
+            pltpu.VMEM((ROWS, 2, ZPIECE, NB), F32),
+            pltpu.VMEM((ROWS, ZPIECE, NB), F32),
             pltpu.VMEM((2, ZPIECE, NB), F32),
             pltpu.VMEM((2, TILE, NB), F32),
             pltpu.VMEM((ZPIECE, NB), F32),
@@ -502,12 +605,17 @@
             pltpu.VMEM((TILE, 512), BF16),
             pltpu.VMEM((512, TILE), BF16),
             dma((4,)),
+            dma((8,)),
+            dma((8,)),
             dma((16,)),
+            dma((8, 2)),
             dma((2,)),
             dma((2,)),
             dma,
             dma((2, 16)),
-            dma,
+            dma((2,)),
+            dma((8, 2)),
+            dma((8,)),
             dma((3, 16)),
             dma((3,)),
             dma((2, 16)),

time: 145 us -> 129 us (0.89)
  Pallas kernels: 139 us -> 122 us
    pallas_call x1, Pallas kernels: 124 us -> 108 us  [body(): pl.pallas_call(exchange, name='exchange', out_shape=(xl_shape, xrt_shape,...]
where the time goes in v2:
time: 129 us; the launch traced here: 128 us
  Pallas kernels  122 us (95%)
  local copies, waits for them, and re-layouts  5.06 us (4%)
    pallas_call x1, Pallas kernels, body(): pl.pallas_call(exchange, name='exchange', out_shape=(xl_shape, xrt_shape,...  108 us
    pallas_call x1, Pallas kernels, body(): pl.pallas_call(update, name='update', grid=(6,), out_shape=(jax.ShapeDtyp...  14.6 us
    unnamed x10, local copies, waits for them, and re-layouts  5.06 us

profile of v2, /device:TPU:0, one launch (start us, length us, event | category | flops | bytes accessed | tf_op | source)
XLA Modules:
  0.0 128.1 jit_solution(16266192078574062327)
XLA Ops:
  0.6 0.0 copy-start.4
  0.6 107.6 %exchange.1 = (bf16[1536,512]{1,0:T(8,128)(2,1)}, bf16[512,1536]{1,0:T(8,128)(2,1)}, bf16[1536,512]{1,0:T(8,128)(2,1)}, bf16[512,1536]{1,0:T(8,128)(2,1)}, f32[16,8,128]{2,1,0:T(8,128)}) custom-call(f32[1536,1536]{1,0:T(8,128)} %mat.3, f32[1,1536]{1,0:T(1,128)} %fard.1, f32[192,128]{1,0:T(8,128)} %vec.1, f32[128,128]{1,0:T(8,128)} %fac.1), custom_call_target="tpu_custom_call" | custom-call | tf_op jit(solution)/shard_map/exchange/pallas_call | solution.py:573
  108.3 0.0 copy-done.4
  108.3 0.0 copy-start
  108.3 1.4 %copy-done = bf16[1536,512]{1,0:T(8,128)(2,1)S(1)} copy-done((bf16[1536,512]{1,0:T(8,128)(2,1)S(1)}, bf16[1536,512]{1,0:T(8,128)(2,1)}, u32[]{:S(2)}) %copy-start) | copy-done | bytes 1572888
  109.7 0.0 copy-start.1
  109.7 1.4 %copy-done.1 = bf16[512,1536]{1,0:T(8,128)(2,1)S(1)} copy-done((bf16[512,1536]{1,0:T(8,128)(2,1)S(1)}, bf16[512,1536]{1,0:T(8,128)(2,1)}, u32[]{:S(2)}) %copy-start.1) | copy-done | bytes 1572888
  111.1 0.0 copy-start.2
  111.1 1.4 %copy-done.2 = bf16[1536,512]{1,0:T(8,128)(2,1)S(1)} copy-done((bf16[1536,512]{1,0:T(8,128)(2,1)S(1)}, bf16[1536,512]{1,0:T(8,128)(2,1)}, u32[]{:S(2)}) %copy-start.2) | copy-done | bytes 1572888
  112.5 0.0 copy-start.3
  112.5 0.8 copy-done.3
  113.4 14.6 %update.1 = (f32[1536,1536]{1,0:T(8,128)}, f32[1,1536]{1,0:T(1,128)}) custom-call(f32[1536,1536]{1,0:T(8,128)} %mat.3, bf16[1536,512]{1,0:T(8,128)(2,1)S(1)} %copy-done, bf16[512,1536]{1,0:T(8,128)(2,1)S(1)} %copy-done.1, f32[16,8,128]{2,1,0:T(8,128)S(1)} %copy-done.3, f32[1,1536]{1,0:T(1,128)S(1)} %copy-done.4, bf16[1536,512]{1,0:T(8,128)(2,1)S(1)} %copy-done.2, ...), custom_call_target="tpu_custom_call" | custom-call | tf_op jit(solution)/shard_map/update/pallas_call | solution.py:632
Async XLA Ops:
  0.6 107.6 %copy-start.4 = (f32[1,1536]{1,0:T(1,128)S(1)}, f32[1,1536]{1,0:T(1,128)}, u32[]{:S(2)}) copy-start(f32[1,1536]{1,0:T(1,128)} %fard.1) | copy-start | bytes 18436
  108.3 1.4 %copy-start = (bf16[1536,512]{1,0:T(8,128)(2,1)S(1)}, bf16[1536,512]{1,0:T(8,128)(2,1)}, u32[]{:S(2)}) copy-start(bf16[1536,512]{1,0:T(8,128)(2,1)} %get-tuple-element.7.xl) | copy-start | bytes 4718596
  109.7 1.4 %copy-start.1 = (bf16[512,1536]{1,0:T(8,128)(2,1)S(1)}, bf16[512,1536]{1,0:T(8,128)(2,1)}, u32[]{:S(2)}) copy-start(bf16[512,1536]{1,0:T(8,128)(2,1)} %get-tuple-element.8.xrt) | copy-start | bytes 4718596
  111.1 1.4 %copy-start.2 = (bf16[1536,512]{1,0:T(8,128)(2,1)S(1)}, bf16[1536,512]{1,0:T(8,128)(2,1)}, u32[]{:S(2)}) copy-start(bf16[1536,512]{1,0:T(8,128)(2,1)} %get-tuple-element.10.xl1_hbm) | copy-start | bytes 4718596
  112.5 0.8 copy-start.3

commit v3 on v2

v3 whole, which is shorter than its diff:
```python
import functools

import jax
import jax.numpy as jnp
from jax import lax
from jax.experimental import pallas as pl
from jax.experimental.pallas import tpu as pltpu
from jax.sharding import PartitionSpec as P

TILE = 1536
NB = 128
GRID = 16
HALF = 8
ROWS = 8
LINE = ((0, 1), (1, 0), (3, 0), (1, 1), (3, 1), (2, 0), (2, 1))
COLS = 16
VPIECE = 192
ZPIECE = 96
WIDTH = 256
PEERS = ((0, 0), (0, 1), (1, 0), (0, 3), (3, 0), (1, 1), (3, 3), (1, 3), (3, 1), (0, 2), (2, 0),
         (2, 1), (1, 2), (2, 3), (3, 2), (2, 2))
MESH = pl.DeviceIdType.MESH
F32 = jnp.float32
BF16 = jnp.bfloat16


def dot(left, right):
    return lax.dot_general(left, right, (((1,), (0,)), ((), ())), preferred_element_type=F32)


def dot_exact(left, right, dims=((1,), (0,))):
    return lax.dot_general(
        left, right, (dims, ((), ())), preferred_element_type=F32, precision=lax.Precision.HIGHEST
    )


def halves(value):
    high = value.astype(BF16)
    low = (value - high.astype(F32)).astype(BF16)
    return high, low


def choose(j, values):
    out = jnp.int32(values[0])
    for k, value in enumerate(values):
        if k > 0 and value != values[0]:
            out = jnp.where(j == k, value, out)
    return out


def put(src, dst, send_sem, recv_sem, to_row, to_col, row, col):
    here = jnp.logical_and(to_row == row, to_col == col)

    @pl.when(here)
    def _():
        pltpu.make_async_copy(src, dst, recv_sem).start()

    @pl.when(jnp.logical_not(here))
    def _():
        pltpu.make_async_remote_copy(
            src_ref=src, dst_ref=dst, send_sem=send_sem, recv_sem=recv_sem,
            device_id=(to_row, to_col), device_id_type=MESH,
        ).start()


def sent(src, dst, send_sem, recv_sem, to_row, to_col, row, col):
    here = jnp.logical_and(to_row == row, to_col == col)

    @pl.when(jnp.logical_not(here))
    def _():
        pltpu.make_async_remote_copy(
            src_ref=src, dst_ref=src, send_sem=send_sem, recv_sem=send_sem,
            device_id=(to_row, to_col), device_id_type=MESH,
        ).wait_send()


def arrived(ref, sem):
    pltpu.make_async_copy(ref, ref, sem).wait()


def exchange(
    mat, lowd, vec, fac, x_out, d_out,
    abuf, bhi, blo, vline, vbuf, vcat, vtc, z, zt, parts, lpart, lsend, zsum, zf, vd,
    gpart, g1, g1s, g2, g2s, gf, dmine, xbuf,
    a_sem, vl_send, vl_recv, vf_send, vo_send, v_recv, vd_send, vd_recv, r_send, r_recv,
    l_send, l_recv, g_send, g_recv, z_send, z_recv, d_send, d_recv, o_sem,
):
    row = lax.axis_index("row")
    col = lax.axis_index("col")
    diag = row == col
    plain = row != col
    other = jnp.where(col < row, col, jnp.where(diag, GRID - 1 - row, col - row - 1))
    far = GRID - 1 - row
    x, core = row // 2, lax.rem(row, 2)

    sign = 1 - 2 * core

    def peer(j):
        z = lax.rem(col // 4 + sign * choose(j, [p[0] for p in PEERS]) + 4, 4)
        y = lax.rem(lax.rem(col, 4) + sign * choose(j, [p[1] for p in PEERS]) + 4, 4)
        return z * 4 + y

    def line_row(step):
        return lax.rem(x + step[0], 4) * 2 + lax.rem(core + step[1], 2)

    def part_copy(k):
        return pltpu.make_async_copy(
            mat.at[pl.ds(k * 384, 384)], abuf.at[pl.ds(k * 384, 384)], a_sem.at[k]
        )

    for k in range(4):
        part_copy(k).start()

    bar = pltpu.get_barrier_semaphore()

    def greet(j, carry):
        pl.semaphore_signal(
            bar, inc=1, device_id=(row, lax.rem(col + j, COLS)), device_id_type=MESH
        )
        return carry

    lax.fori_loop(1, COLS, greet, 0)
    for step in LINE:
        pl.semaphore_signal(bar, inc=1, device_id=(line_row(step), col), device_id_type=MESH)

    own = pltpu.make_async_copy(vec, vline.at[row], vl_recv.at[row])
    own.start()

    def split_part(k):
        part_copy(k).wait()

        @pl.when(plain)
        def _():
            def split(s, carry):
                rows = pl.ds(pl.multiple_of(k * 384 + s * 32, 32), 32)
                high, low = halves(abuf[rows, :])
                bhi[0, rows, :] = high
                blo[0, rows, :] = low
                return carry

            lax.fori_loop(0, 12, split, 0)

    split_part(0)
    split_part(1)
    pl.semaphore_wait(bar, COLS - 1 + ROWS - 1)

    vtile = 2 * row + col // 8
    vpiece = lax.rem(col, 8)
    parity = col // 8
    vlead_row = jnp.where(vtile < HALF, vtile, GRID - 1 - vtile)

    def v_line(j, to_row):
        return pltpu.make_async_remote_copy(
            src_ref=vec, dst_ref=vline.at[row], send_sem=vl_send.at[j],
            recv_sem=vl_recv.at[row], device_id=(to_row, col), device_id_type=MESH,
        )

    def v_line_lead(act):
        @pl.when(vlead_row != row)
        def _():
            act(v_line(7, vlead_row))

    def v_line_each(act):
        for j, step in enumerate(LINE):
            to_row = line_row(step)

            @pl.when(jnp.logical_and(to_row != vlead_row, to_row <= GRID - 1 - vtile))
            def _():
                act(v_line(j, to_row))

    v_line_lead(lambda copy: copy.start())

    lead_near = lax.rem(row, 2) == parity
    lead_src = jnp.where(lead_near, row, far) // 2
    v_rows = pl.ds(vpiece * VPIECE, VPIECE)

    def v_lead_each(act):
        def one(j, carry):
            c = peer(j)

            @pl.when(jnp.logical_or(c == row, (c < row) == lead_near))
            def _():
                slot = jnp.where(jnp.logical_and(c == row, lead_near), 1, 0)
                act(vline.at[lead_src], vbuf.at[slot, v_rows], vf_send.at[j], v_recv.at[slot],
                    row, c, row, col)

            return carry

        lax.fori_loop(0, COLS, one, 0)

        @pl.when(jnp.logical_not(lead_near))
        def _():
            for k in range(2):
                act(vline.at[lead_src, pl.ds(k * ZPIECE, ZPIECE)], vd, vd_send.at[k], vd_recv,
                    row, 2 * vpiece + k, row, col)

    def v_other_each(act, before):
        for j, step in enumerate(((0, 0),) + LINE):
            src = line_row(step)
            tile = 2 * src + parity

            @pl.when(jnp.logical_and(tile <= far, src != lead_src))
            def _():
                before(src)

            @pl.when(tile < row)
            def _():
                act(vline.at[src], vbuf.at[1, v_rows], vo_send.at[j, 0], v_recv.at[1],
                    row, tile, row, col)

            @pl.when(tile < far)
            def _():
                act(vline.at[src], vbuf.at[1, v_rows], vo_send.at[j, 1], v_recv.at[1],
                    row, tile + row + 1, row, col)

    arrived(vline.at[lead_src], vl_recv.at[lead_src])
    v_lead_each(put)
    v_line_each(lambda copy: copy.start())
    v_other_each(put, lambda src: arrived(vline.at[src], vl_recv.at[src]))

    @pl.when(jnp.logical_and(vtile > far, lead_src != row))
    def _():
        arrived(vline.at[row], vl_recv.at[row])

    split_part(2)
    split_part(3)

    @pl.when(diag)
    def _():
        def keep(s, rows, cols, value):
            high, low = halves(value)
            bhi[s, rows, cols] = high
            blo[s, rows, cols] = low

        def block_at(n, carry):
            p, q = n // 6, lax.rem(n, 6)
            rows = pl.ds(pl.multiple_of(p * 256, 256), 256)
            cols = pl.ds(pl.multiple_of(q * 256, 256), 256)

            @pl.when(p != q)
            def _():
                s = jnp.where(p > q, 0, 1)
                block = abuf[rows, cols]
                keep(s, rows, cols, block)
                keep(s, cols, rows, block.T)

            @pl.when(p == q)
            def _():
                block = abuf[rows, cols]
                rr = lax.broadcasted_iota(jnp.int32, (256, 256), 0)
                cc = lax.broadcasted_iota(jnp.int32, (256, 256), 1)
                lower = jnp.where(rr > cc, block, 0.0)
                upper = jnp.where(rr < cc, block, 0.0)
                onto = jnp.where(rr == cc, block, 0.0)
                far_onto = jnp.where(rr == cc, jnp.broadcast_to(lowd[:, cols], (256, 256)), 0.0)
                keep(0, rows, cols, lower + lower.T + onto)
                keep(1, rows, cols, upper + upper.T + far_onto)

            return carry

        lax.fori_loop(0, 36, block_at, 0)

    def cat_v(s):
        for p in range(6):
            at = slice(p * 256, p * 256 + 256)
            high, low = halves(vbuf[s, at, :])
            vcat[s, at, 0:128] = high
            vcat[s, at, 128:256] = low

    def cat_vt(s):
        for p in range(6):
            at = slice(p * 256, p * 256 + 256)
            high, low = halves(vbuf[s, at, :].T)
            vtc[s, 0:128, at] = high
            vtc[s, 128:256, at] = low

    def times(high, low, v):
        full = dot(high, v)
        return full[:, 0:128] + full[:, 128:256] + dot(low, v[:, 0:128])

    def times_t(vt, high, low):
        full = dot(vt, high)
        return full[0:128] + full[128:256] + dot(vt[0:128], low)

    def z_put(s, act=put):
        def one(j, carry):
            c = peer(j)
            act(z.at[s, pl.ds(c * ZPIECE, ZPIECE)], parts.at[s, col], r_send.at[s, c],
                r_recv.at[s], row, c, row, col)
            return carry

        lax.fori_loop(0, COLS, one, 0)

    def g_start():
        def one(j, carry):
            c = lax.rem(j + col, COLS)
            put(gpart.at[pl.ds(pl.multiple_of(c * 8, 8), 8)], g1.at[col], g_send.at[0, c],
                g_recv.at[0], row, c, row, col)
            return carry

        lax.fori_loop(0, COLS, one, 0)

    second = jnp.where(diag, 1, 0)
    arrived(vbuf.at[0], v_recv.at[0])
    cat_vt(0)

    def turned_panel(k, carry):
        at = pl.ds(pl.multiple_of(k * 768, 768), 768)
        part = times_t(vtc[0], bhi[second, :, at], blo[second, :, at])
        zt[:, at] = part
        z[1, at, :] = part.T
        return carry

    lax.fori_loop(0, 2, turned_panel, 0)
    z_put(1)

    arrived(vbuf.at[1], v_recv.at[1])
    cat_v(1)

    @pl.when(plain)
    def _():
        high, low = halves(zt[...])
        y = times(high, low, vcat[1])
        gpart[...] = y + y.T
        g_start()

    def panel(k, carry):
        rows = pl.ds(pl.multiple_of(k * 384, 384), 384)
        z[0, rows, :] = times(bhi[0, rows, :], blo[0, rows, :], vcat[1])
        return carry

    lax.fori_loop(0, 4, panel, 0)
    z_put(0)

    @pl.when(diag)
    def _():
        cat_v(0)
        cat_vt(1)
        high, low = halves(zt[...])
        y = times(high, low, vcat[0])
        high, low = halves(z[0])
        full = dot(vtc[1], high)
        gpart[...] = y + full[0:128] + full[128:256] + dot(vtc[1, 0:128, :], low)
        g_start()

    arrived(parts.at[1], r_recv.at[1])
    for step in LINE:
        to = line_row(step)

        @pl.when(to < row)
        def _():
            lsend[to] = parts[1, to] + parts[1, to + row + 1]

    def l_copy(src, to, k):
        return pltpu.make_async_remote_copy(
            src_ref=src, dst_ref=lpart.at[row, k], send_sem=l_send.at[to, k],
            recv_sem=l_recv.at[row], device_id=(to, col), device_id_type=MESH,
        )

    def l_each(act):
        for step in LINE:
            to = line_row(step)

            @pl.when(to < row)
            def _():
                act(l_copy(lsend.at[to], to, 0))

            @pl.when(to > row)
            def _():
                act(l_copy(parts.at[1, to + row + 1], to, 0))
                act(l_copy(parts.at[1, GRID - to + row], to, 1))

    l_each(lambda copy: copy.start())

    arrived(g1, g_recv.at[0])
    g1s[...] = jnp.sum(g1[...], axis=0)

    def g_line(j, carry):
        r = lax.rem(j + row, ROWS)
        put(g1s, g2.at[row], g_send.at[1, r], g_recv.at[1], r, col, row, col)
        return carry

    lax.fori_loop(0, ROWS, g_line, 0)

    arrived(parts.at[0], r_recv.at[0])
    zsum[0] = parts[1, 2 * row + 1]
    zsum[1] = parts[1, row]

    def add_lead(c, carry):
        zsum[jnp.where(c <= row, 0, 1)] += parts[0, c]
        return carry

    lax.fori_loop(0, COLS, add_lead, 0)
    for step in LINE:
        src = line_row(step)

        @pl.when(src < row)
        def _():
            arrived(lpart.at[src], l_recv.at[src])
            zsum[0] += lpart[src, 0]
            zsum[1] += lpart[src, 1]

        @pl.when(src > row)
        def _():
            arrived(lpart.at[src, 0], l_recv.at[src])
            zsum[0] += lpart[src, 0]

    arrived(g2, g_recv.at[1])
    g2s[...] = jnp.sum(g2[...], axis=0)

    def g_row(j, carry):
        c = lax.rem(j + col, COLS)
        put(g2s, gf.at[pl.ds(pl.multiple_of(col * 8, 8), 8)], g_send.at[2, c], g_recv.at[2],
            row, c, row, col)
        return carry

    lax.fori_loop(0, COLS, g_row, 0)

    def zf_each(act):
        def one(j, carry):
            c = peer(j)
            half = jnp.where(c <= row, 0, 1)
            slot = jnp.where(c == row, 1, 0)
            act(zsum.at[half], zf.at[slot, pl.ds(col * ZPIECE, ZPIECE)], z_send.at[0, j],
                z_recv.at[slot], row, c, row, col)
            to = lax.rem(row + sign * j + 2 * ROWS, ROWS)
            first = j < ROWS
            half = jnp.where(jnp.logical_or(first, to > row), 0, 1)
            slot = jnp.where(jnp.logical_or(first, to != row), 1, 0)
            to_col = jnp.where(
                first, to + row + 1, jnp.where(to >= row, row, GRID - row + to))
            act(zsum.at[half], zf.at[slot, pl.ds(col * ZPIECE, ZPIECE)], z_send.at[1, j],
                z_recv.at[slot], to, to_col, row, col)
            return carry

        lax.fori_loop(0, COLS, one, 0)

    zf_each(put)

    arrived(gf, g_recv.at[2])
    fac_value = fac[...]
    middle = dot_exact(dot_exact(fac_value, gf[...], ((0,), (0,))), fac_value)

    arrived(vd, vd_recv)
    v_far = vd[...]
    w_far = dot_exact(zsum[1], fac_value) - 0.5 * dot_exact(v_far, middle)
    sums = dot_exact(jnp.ones((8, 128), F32), v_far * w_far, ((1,), (1,)))
    dmine[...] = jnp.concatenate([sums, jnp.zeros((8, 32), F32)], axis=1)

    def d_put(j, carry):
        c = lax.rem(j + col, COLS)
        put(dmine, d_out.at[col], d_send.at[c], d_recv, row, c, row, col)
        return carry

    lax.fori_loop(0, COLS, d_put, 0)

    both = jnp.concatenate([fac_value, -0.5 * middle], axis=0)
    both_high, both_low = halves(both)

    def w_into(s):
        def panel(k, carry):
            rows = pl.ds(pl.multiple_of(k * 256, 256), 256)
            v_high, v_low = halves(vbuf[s, rows, :])
            z_high, z_low = halves(zf[s, rows, :])
            high = jnp.concatenate([z_high, v_high], axis=1)
            low = jnp.concatenate([z_low, v_low], axis=1)
            w = dot(high, both_high) + dot(high, both_low) + dot(low, both_high)
            w_high, w_low = halves(w)
            xbuf[s, rows, :] = jnp.concatenate([v_high, w_high, v_low, w_low], axis=1)
            return carry

        lax.fori_loop(0, 6, panel, 0)
        pltpu.make_async_copy(xbuf.at[s], x_out.at[s], o_sem.at[s]).start()

    for s in (1, 0):
        arrived(zf.at[s], z_recv.at[s])
        w_into(s)

    arrived(d_out, d_recv)

    v_line_lead(lambda copy: copy.wait_send())
    v_line_each(lambda copy: copy.wait_send())
    v_lead_each(sent)
    v_other_each(sent, lambda src: None)
    z_put(0, sent)
    z_put(1, sent)
    l_each(lambda copy: copy.wait_send())

    zf_each(sent)

    def all_sent(j, carry):
        sent(g1s, g1s, g_send.at[0, j], None, row, j, row, col)
        sent(g2s, g2s, g_send.at[2, j], None, row, j, row, col)
        sent(dmine, dmine, d_send.at[j], None, row, j, row, col)
        return carry

    lax.fori_loop(0, 16, all_sent, 0)

    def line_sent(j, carry):
        sent(g1s, g1s, g_send.at[1, j], None, j, col, row, col)
        return carry

    lax.fori_loop(0, ROWS, line_sent, 0)

    arrived(xbuf.at[0], o_sem.at[0])
    arrived(xbuf.at[1], o_sem.at[1])


def update(mat, x_hbm, d, fard, out, far_out, abuf, x, sem, in_sem, out_sem):
    diag = lax.axis_index("row") == lax.axis_index("col")
    x_copy = pltpu.make_async_copy(x_hbm, x, sem)
    x_copy.start()

    def columns(k):
        return pl.ds(pl.multiple_of(k * WIDTH, WIDTH), WIDTH)

    def load(k):
        return pltpu.make_async_copy(mat.at[:, columns(k)], abuf.at[:, columns(k)], in_sem.at[k])

    def store(k):
        return pltpu.make_async_copy(abuf.at[:, columns(k)], out.at[:, columns(k)], out_sem.at[k])

    def each(act):
        def one(k, carry):
            act(k)
            return carry

        lax.fori_loop(0, TILE // WIDTH, one, 0)

    each(lambda k: load(k).start())

    lane = lax.broadcasted_iota(jnp.int32, (128, TILE), 1)
    start = jnp.zeros((128, TILE), jnp.int32)
    for k in range(1, 16):
        start += jnp.where(lane >= k * ZPIECE, ZPIECE, 0)
    pick = jnp.where(lane - start == lax.broadcasted_iota(jnp.int32, (128, TILE), 0), 1.0, 0.0)
    spread = dot_exact(d[:, 0, :], pick)
    piece = lax.broadcasted_iota(jnp.int32, (16, TILE), 0) * ZPIECE
    whole = jnp.sum(jnp.where(piece == start[0:16], spread, 0.0), axis=0, keepdims=True)
    far_out[...] = fard[...] - 2.0 * whole
    x_copy.wait()

    def dot_nt(left, right):
        return lax.dot_general(
            left, right, (((1,), (1,)), ((), ())), preferred_element_type=F32
        )

    def change(s, t, cols, rows=slice(None)):
        v_high, w_high = x[t, cols, 0:128], x[t, cols, 128:256]
        v_low, w_low = x[t, cols, 256:384], x[t, cols, 384:512]
        high = jnp.concatenate([w_high, v_high], axis=1)
        low = jnp.concatenate([w_low, v_low], axis=1)
        left_high, left_low = x[s, rows, 0:256], x[s, rows, 256:512]
        return dot_nt(left_high, high) + dot_nt(left_high, low) + dot_nt(left_low, high)

    @pl.when(jnp.logical_not(diag))
    def _():
        def step(k):
            cols = columns(k)
            load(k).wait()
            abuf[:, cols] -= change(0, 1, cols)
            store(k).start()

        each(step)

    @pl.when(diag)
    def _():
        below = lax.broadcasted_iota(jnp.int32, (WIDTH, WIDTH), 0) >= lax.broadcasted_iota(
            jnp.int32, (WIDTH, WIDTH), 1)
        for k in range(TILE // WIDTH):
            lo, hi = k * WIDTH, k * WIDTH + WIDTH
            cols = slice(lo, hi)
            load(k).wait()
            near = change(1, 1, cols, slice(lo, TILE))
            far = change(0, 0, cols, slice(0, hi))
            if k > 0:
                abuf[0:lo, cols] -= far[0:lo]
            abuf[lo:hi, cols] -= jnp.where(below, near[0:WIDTH], far[lo:hi])
            if hi < TILE:
                abuf[hi:, cols] -= near[WIDTH:]
            store(k).start()

    each(lambda k: store(k).wait())


def body(matrix, far_diag, vectors, factors):
    any_spec = pl.BlockSpec(memory_space=pl.ANY)
    vmem_spec = pl.BlockSpec(memory_space=pltpu.VMEM)
    dma = pltpu.SemaphoreType.DMA
    x, d = pl.pallas_call(
        exchange,
        name="exchange",
        out_shape=(jax.ShapeDtypeStruct((2, TILE, 512), BF16),
                   jax.ShapeDtypeStruct((16, 8, 128), F32)),
        in_specs=[any_spec, vmem_spec, vmem_spec, vmem_spec],
        out_specs=(any_spec, vmem_spec),
        scratch_shapes=[
            pltpu.VMEM((TILE, TILE), F32),
            pltpu.VMEM((2, TILE, TILE), BF16),
            pltpu.VMEM((2, TILE, TILE), BF16),
            pltpu.VMEM((ROWS, VPIECE, NB), F32),
            pltpu.VMEM((2, TILE, NB), F32),
            pltpu.VMEM((2, TILE, 2 * NB), BF16),
            pltpu.VMEM((2, 2 * NB, TILE), BF16),
            pltpu.VMEM((2, TILE, NB), F32),
            pltpu.VMEM((NB, TILE), F32),
            pltpu.VMEM((2, COLS, ZPIECE, NB), F32),
            pltpu.VMEM((ROWS, 2, ZPIECE, NB), F32),
            pltpu.VMEM((ROWS, ZPIECE, NB), F32),
            pltpu.VMEM((2, ZPIECE, NB), F32),
            pltpu.VMEM((2, TILE, NB), F32),
            pltpu.VMEM((ZPIECE, NB), F32),
            pltpu.VMEM((NB, NB), F32),
            pltpu.VMEM((16, 8, NB), F32),
            pltpu.VMEM((8, NB), F32),
            pltpu.VMEM((8, 8, NB), F32),
            pltpu.VMEM((8, NB), F32),
            pltpu.VMEM((NB, NB), F32),
            pltpu.VMEM((8, NB), F32),
            pltpu.VMEM((2, TILE, 512), BF16),
            dma((4,)),
            dma((8,)),
            dma((8,)),
            dma((16,)),
            dma((8, 2)),
            dma((2,)),
            dma((2,)),
            dma,
            dma((2, 16)),
            dma((2,)),
            dma((8, 2)),
            dma((8,)),
            dma((3, 16)),
            dma((3,)),
            dma((2, 16)),
            dma((2,)),
            dma((16,)),
            dma,
            dma((2,)),
        ],
        compiler_params=pltpu.CompilerParams(
            collective_id=0, has_side_effects=True, vmem_limit_bytes=56 * 2**20
        ),
    )(matrix, far_diag, vectors, factors)
    updated, far_updated = pl.pallas_call(
        update,
        name="update",
        out_shape=(jax.ShapeDtypeStruct((TILE, TILE), F32), jax.ShapeDtypeStruct((1, TILE), F32)),
        in_specs=[any_spec, any_spec, vmem_spec, vmem_spec],
        out_specs=(any_spec, vmem_spec),
        scratch_shapes=[
            pltpu.VMEM((TILE, TILE), F32),
            pltpu.VMEM((2, TILE, 512), BF16),
            dma,
            dma((TILE // WIDTH,)),
            dma((TILE // WIDTH,)),
        ],
        compiler_params=pltpu.CompilerParams(vmem_limit_bytes=60 * 2**20),
    )(matrix, x, d, far_diag)
    return updated, far_updated


def solution(mesh):
    in_specs = (P("row", "col"), P("row", None), P(("row", "col"), None), P())
    out_specs = (P("row", "col"), P("row", None))
    return jax.shard_map(body, mesh=mesh, in_specs=in_specs, out_specs=out_specs, check_vma=False)
```

time: 129 us -> 110 us (0.85)
  the two profiles are of different devices: /device:TPU:0 before, /device:TPU:36 now
where the time goes in v3:
time: 110 us
  Pallas kernels  109 us (99%)
    pallas_call x1, Pallas kernels, body(): pl.pallas_call(exchange, name='exchange', out_shape=(jax.ShapeDtypeStruct...  96.9 us
    pallas_call x1, Pallas kernels, body(): pl.pallas_call(update, name='update', out_shape=(jax.ShapeDtypeStruct((TI...  12.3 us

profile of v3, /device:TPU:36, one launch (start us, length us, event | category | flops | bytes accessed | tf_op | source)
XLA Modules:
  0.0 110.0 jit_solution(5007250904502925366)
XLA Ops:
  0.6 96.9 %exchange.1 = (bf16[2,1536,512]{2,1,0:T(8,128)(2,1)}, f32[16,8,128]{2,1,0:T(8,128)}) custom-call(f32[1536,1536]{1,0:T(8,128)} %mat.3, f32[1,1536]{1,0:T(1,128)} %fard.1, f32[192,128]{1,0:T(8,128)} %vec.1, f32[128,128]{1,0:T(8,128)} %fac.1), custom_call_target="tpu_custom_call" | custom-call | tf_op jit(solution)/shard_map/exchange/pallas_call | solution.py:590
  97.6 12.3 %update.1 = (f32[1536,1536]{1,0:T(8,128)}, f32[1,1536]{1,0:T(1,128)}) custom-call(f32[1536,1536]{1,0:T(8,128)} %mat.3, bf16[2,1536,512]{2,1,0:T(8,128)(2,1)} %get-tuple-element.4.x_hbm, f32[16,8,128]{2,1,0:T(8,128)} %get-tuple-element.5.d, f32[1,1536]{1,0:T(1,128)} %fard.1), custom_call_target="tpu_custom_call" | custom-call | tf_op jit(solution)/shard_map/update/pallas_call | solution.py:645

commit v4 on v3

--- a/solution.py
+++ b/solution.py
@@ -80,9 +80,9 @@
 
 def exchange(
     mat, lowd, vec, fac, x_out, d_out,
-    abuf, bhi, blo, vline, vbuf, vcat, vtc, z, zt, parts, lpart, lsend, zsum, zf, vd,
+    abuf, bhi, blo, vline, vz, vbuf, vcat, vtc, z, zt, parts, lpart, lsend, zsum, zf, vd,
     gpart, g1, g1s, g2, g2s, gf, dmine, xbuf,
-    a_sem, vl_send, vl_recv, vf_send, vo_send, v_recv, vd_send, vd_recv, r_send, r_recv,
+    a_sem, vl_send, vl_recv, vz_send, vz_recv, vf_send, vo_send, v_recv, vd_send, vd_recv, r_send, r_recv,
     l_send, l_recv, g_send, g_recv, z_send, z_recv, d_send, d_recv, o_sem,
 ):
     row = lax.axis_index("row")
@@ -174,19 +174,17 @@
     lead_src = jnp.where(lead_near, row, far) // 2
     v_rows = pl.ds(vpiece * VPIECE, VPIECE)
 
+    z_at, y_at = col // 4, lax.rem(col, 4)
+    z_row = row // 4
+
     def v_lead_each(act):
-        def one(j, carry):
-            c = peer(j)
-
-            @pl.when(jnp.logical_or(c == row, (c < row) == lead_near))
-            def _():
-                slot = jnp.where(jnp.logical_and(c == row, lead_near), 1, 0)
-                act(vline.at[lead_src], vbuf.at[slot, v_rows], vf_send.at[j], v_recv.at[slot],
-                    row, c, row, col)
-
-            return carry
-
-        lax.fori_loop(0, COLS, one, 0)
+        for j, dz in enumerate((0, 1, 3, 2)):
+            to_z = lax.rem(z_at + sign * dz + 4, 4)
+
+            @pl.when(jnp.logical_or(to_z == z_row, (to_z < z_row) == lead_near))
+            def _():
+                act(vline.at[lead_src], vz.at[z_at], vz_send.at[j], vz_recv.at[z_at],
+                    row, to_z * 4 + y_at, row, col)
 
         @pl.when(jnp.logical_not(lead_near))
         def _():
@@ -194,8 +192,27 @@
                 act(vline.at[lead_src, pl.ds(k * ZPIECE, ZPIECE)], vd, vd_send.at[k], vd_recv,
                     row, 2 * vpiece + k, row, col)
 
-    def v_other_each(act, before):
-        for j, step in enumerate(((0, 0),) + LINE):
+    def v_hand_each(act, before):
+        for j, dz in enumerate((0, 1, 3, 2)):
+            src = lax.rem(z_at - sign * dz + 4, 4)
+            near = lax.rem(row, 2) == src // 2
+
+            @pl.when(jnp.logical_or(z_at == z_row, (z_at < z_row) == near))
+            def _():
+                before(src)
+
+                for i, dy in enumerate((0, 1, 3, 2)):
+                    c = z_at * 4 + lax.rem(y_at + sign * dy + 4, 4)
+
+                    @pl.when(jnp.logical_or(c == row, (c < row) == near))
+                    def _():
+                        slot = jnp.where(jnp.logical_and(c == row, near), 1, 0)
+                        rows = pl.ds((lax.rem(src, 2) * 4 + y_at) * VPIECE, VPIECE)
+                        act(vz.at[src], vbuf.at[slot, rows], vf_send.at[j, i], v_recv.at[slot],
+                            row, c, row, col)
+
+    def v_other_each(act, before, first_j=0, last_j=ROWS):
+        for j, step in list(enumerate(((0, 0),) + LINE))[first_j:last_j]:
             src = line_row(step)
             tile = 2 * src + parity
 
@@ -205,18 +222,20 @@
 
             @pl.when(tile < row)
             def _():
-                act(vline.at[src], vbuf.at[1, v_rows], vo_send.at[j, 0], v_recv.at[1],
+                act(vec if j == 0 else vline.at[src], vbuf.at[1, v_rows], vo_send.at[j, 0], v_recv.at[1],
                     row, tile, row, col)
 
             @pl.when(tile < far)
             def _():
-                act(vline.at[src], vbuf.at[1, v_rows], vo_send.at[j, 1], v_recv.at[1],
+                act(vec if j == 0 else vline.at[src], vbuf.at[1, v_rows], vo_send.at[j, 1], v_recv.at[1],
                     row, tile + row + 1, row, col)
 
+    v_other_each(put, lambda src: arrived(vline.at[src], vl_recv.at[src]), 0, 1)
     arrived(vline.at[lead_src], vl_recv.at[lead_src])
     v_lead_each(put)
     v_line_each(lambda copy: copy.start())
-    v_other_each(put, lambda src: arrived(vline.at[src], vl_recv.at[src]))
+    v_hand_each(put, lambda src: arrived(vz.at[src], vz_recv.at[src]))
+    v_other_each(put, lambda src: arrived(vline.at[src], vl_recv.at[src]), 1)
 
     @pl.when(jnp.logical_and(vtile > far, lead_src != row))
     def _():
@@ -282,11 +301,15 @@
         full = dot(vt, high)
         return full[0:128] + full[128:256] + dot(vt[0:128], low)
 
-    def z_put(s, act=put):
+    def z_put(s, act=put, half=None):
         def one(j, carry):
             c = peer(j)
-            act(z.at[s, pl.ds(c * ZPIECE, ZPIECE)], parts.at[s, col], r_send.at[s, c],
-                r_recv.at[s], row, c, row, col)
+
+            @pl.when(True if half is None else c // 8 == half)
+            def _():
+                act(z.at[s, pl.ds(c * ZPIECE, ZPIECE)], parts.at[s, col], r_send.at[s, c],
+                    r_recv.at[s], row, c, row, col)
+
             return carry
 
         lax.fori_loop(0, COLS, one, 0)
@@ -304,15 +327,16 @@
     arrived(vbuf.at[0], v_recv.at[0])
     cat_vt(0)
 
-    def turned_panel(k, carry):
+    def turned_panel(n, carry):
+        k = lax.rem(n + z_at // 2, 2)
         at = pl.ds(pl.multiple_of(k * 768, 768), 768)
         part = times_t(vtc[0], bhi[second, :, at], blo[second, :, at])
         zt[:, at] = part
         z[1, at, :] = part.T
+        z_put(1, half=k)
         return carry
 
     lax.fori_loop(0, 2, turned_panel, 0)
-    z_put(1)
 
     arrived(vbuf.at[1], v_recv.at[1])
     cat_v(1)
@@ -324,13 +348,14 @@
         gpart[...] = y + y.T
         g_start()
 
-    def panel(k, carry):
-        rows = pl.ds(pl.multiple_of(k * 384, 384), 384)
+    def panel(n, carry):
+        k = lax.rem(n + z_at // 2, 2)
+        rows = pl.ds(pl.multiple_of(k * 768, 768), 768)
         z[0, rows, :] = times(bhi[0, rows, :], blo[0, rows, :], vcat[1])
-        return carry
-
-    lax.fori_loop(0, 4, panel, 0)
-    z_put(0)
+        z_put(0, half=k)
+        return carry
+
+    lax.fori_loop(0, 2, panel, 0)
 
     @pl.when(diag)
     def _():
@@ -405,24 +430,13 @@
             arrived(lpart.at[src, 0], l_recv.at[src])
             zsum[0] += lpart[src, 0]
 
-    arrived(g2, g_recv.at[1])
-    g2s[...] = jnp.sum(g2[...], axis=0)
-
-    def g_row(j, carry):
-        c = lax.rem(j + col, COLS)
-        put(g2s, gf.at[pl.ds(pl.multiple_of(col * 8, 8), 8)], g_send.at[2, c], g_recv.at[2],
-            row, c, row, col)
-        return carry
-
-    lax.fori_loop(0, COLS, g_row, 0)
-
-    def zf_each(act):
+    def zf_each(first_j, last_j, act):
         def one(j, carry):
             c = peer(j)
             half = jnp.where(c <= row, 0, 1)
             slot = jnp.where(c == row, 1, 0)
             act(zsum.at[half], zf.at[slot, pl.ds(col * ZPIECE, ZPIECE)], z_send.at[0, j],
-                z_recv.at[slot], row, c, row, col)
+                z_recv.at[slot, z_at], row, c, row, col)
             to = lax.rem(row + sign * j + 2 * ROWS, ROWS)
             first = j < ROWS
             half = jnp.where(jnp.logical_or(first, to > row), 0, 1)
@@ -430,12 +444,23 @@
             to_col = jnp.where(
                 first, to + row + 1, jnp.where(to >= row, row, GRID - row + to))
             act(zsum.at[half], zf.at[slot, pl.ds(col * ZPIECE, ZPIECE)], z_send.at[1, j],
-                z_recv.at[slot], to, to_col, row, col)
+                z_recv.at[slot, z_at], to, to_col, row, col)
             return carry
 
-        lax.fori_loop(0, COLS, one, 0)
-
-    zf_each(put)
+        lax.fori_loop(first_j, last_j, one, 0)
+
+    zf_each(0, 6, put)
+    arrived(g2, g_recv.at[1])
+    g2s[...] = jnp.sum(g2[...], axis=0)
+
+    def g_row(j, carry):
+        c = lax.rem(j + col, COLS)
+        put(g2s, gf.at[pl.ds(pl.multiple_of(col * 8, 8), 8)], g_send.at[2, c], g_recv.at[2],
+            row, c, row, col)
+        return carry
+
+    lax.fori_loop(0, COLS, g_row, 0)
+    zf_each(6, COLS, put)
 
     arrived(gf, g_recv.at[2])
     fac_value = fac[...]
@@ -457,9 +482,12 @@
     both = jnp.concatenate([fac_value, -0.5 * middle], axis=0)
     both_high, both_low = halves(both)
 
-    def w_into(s):
-        def panel(k, carry):
-            rows = pl.ds(pl.multiple_of(k * 256, 256), 256)
+    def w_into(step):
+        k = lax.rem(z_at + step, 4)
+
+        def one(s, carry):
+            rows = pl.ds(pl.multiple_of(k * 384, 384), 384)
+            arrived(zf.at[s, rows], z_recv.at[s, k])
             v_high, v_low = halves(vbuf[s, rows, :])
             z_high, z_low = halves(zf[s, rows, :])
             high = jnp.concatenate([z_high, v_high], axis=1)
@@ -467,26 +495,26 @@
             w = dot(high, both_high) + dot(high, both_low) + dot(low, both_high)
             w_high, w_low = halves(w)
             xbuf[s, rows, :] = jnp.concatenate([v_high, w_high, v_low, w_low], axis=1)
+            pltpu.make_async_copy(xbuf.at[s, rows], x_out.at[s, rows], o_sem.at[s, k]).start()
             return carry
 
-        lax.fori_loop(0, 6, panel, 0)
-        pltpu.make_async_copy(xbuf.at[s], x_out.at[s], o_sem.at[s]).start()
-
-    for s in (1, 0):
-        arrived(zf.at[s], z_recv.at[s])
-        w_into(s)
+        lax.fori_loop(0, 2, one, 0)
+
+    for step in (0, 1, 3, 2):
+        w_into(step)
 
     arrived(d_out, d_recv)
 
     v_line_lead(lambda copy: copy.wait_send())
     v_line_each(lambda copy: copy.wait_send())
     v_lead_each(sent)
+    v_hand_each(sent, lambda src: None)
     v_other_each(sent, lambda src: None)
     z_put(0, sent)
     z_put(1, sent)
     l_each(lambda copy: copy.wait_send())
 
-    zf_each(sent)
+    zf_each(0, COLS, sent)
 
     def all_sent(j, carry):
         sent(g1s, g1s, g_send.at[0, j], None, row, j, row, col)
@@ -502,8 +530,9 @@
 
     lax.fori_loop(0, ROWS, line_sent, 0)
 
-    arrived(xbuf.at[0], o_sem.at[0])
-    arrived(xbuf.at[1], o_sem.at[1])
+    for s in range(2):
+        for k in range(4):
+            arrived(xbuf.at[s, pl.ds(k * 384, 384)], o_sem.at[s, k])
 
 
 def update(mat, x_hbm, d, fard, out, far_out, abuf, x, sem, in_sem, out_sem):
@@ -599,6 +628,7 @@
             pltpu.VMEM((2, TILE, TILE), BF16),
             pltpu.VMEM((2, TILE, TILE), BF16),
             pltpu.VMEM((ROWS, VPIECE, NB), F32),
+            pltpu.VMEM((4, VPIECE, NB), F32),
             pltpu.VMEM((2, TILE, NB), F32),
             pltpu.VMEM((2, TILE, 2 * NB), BF16),
             pltpu.VMEM((2, 2 * NB, TILE), BF16),
@@ -621,7 +651,9 @@
             dma((4,)),
             dma((8,)),
             dma((8,)),
-            dma((16,)),
+            dma((4,)),
+            dma((4,)),
+            dma((4, 4)),
             dma((8, 2)),
             dma((2,)),
             dma((2,)),
@@ -633,10 +665,10 @@
             dma((3, 16)),
             dma((3,)),
             dma((2, 16)),
-            dma((2,)),
+            dma((2, 4)),
             dma((16,)),
             dma,
-            dma((2,)),
+            dma((2, 4)),
         ],
         compiler_params=pltpu.CompilerParams(
             collective_id=0, has_side_effects=True, vmem_limit_bytes=56 * 2**20

time: 110 us -> 105 us (0.955)
  the two profiles are of different devices: /device:TPU:36 before, /device:TPU:0 now
where the time goes in v4:
time: 105 us
  Pallas kernels  104 us (99%)
    pallas_call x1, Pallas kernels, body(): pl.pallas_call(exchange, name='exchange', out_shape=(jax.ShapeDtypeStruct...  91.5 us
    pallas_call x1, Pallas kernels, body(): pl.pallas_call(update, name='update', out_shape=(jax.ShapeDtypeStruct((TI...  12.3 us

profile of v4, /device:TPU:0, one launch (start us, length us, event | category | flops | bytes accessed | tf_op | source)
XLA Modules:
  0.0 104.6 jit_solution(13849578086466628036)
XLA Ops:
  0.6 91.5 %exchange.1 = (bf16[2,1536,512]{2,1,0:T(8,128)(2,1)}, f32[16,8,128]{2,1,0:T(8,128)}) custom-call(f32[1536,1536]{1,0:T(8,128)} %mat.3, f32[1,1536]{1,0:T(1,128)} %fard.1, f32[192,128]{1,0:T(8,128)} %vec.1, f32[128,128]{1,0:T(8,128)} %fac.1), custom_call_target="tpu_custom_call" | custom-call | tf_op jit(solution)/shard_map/exchange/pallas_call | solution.py:619
  92.1 12.3 %update.1 = (f32[1536,1536]{1,0:T(8,128)}, f32[1,1536]{1,0:T(1,128)}) custom-call(f32[1536,1536]{1,0:T(8,128)} %mat.3, bf16[2,1536,512]{2,1,0:T(8,128)(2,1)} %get-tuple-element.4.x_hbm, f32[16,8,128]{2,1,0:T(8,128)} %get-tuple-element.5.d, f32[1,1536]{1,0:T(1,128)} %fard.1), custom_call_target="tpu_custom_call" | custom-call | tf_op jit(solution)/shard_map/update/pallas_call | solution.py:677

commit v5 on v4

--- a/solution.py
+++ b/solution.py
@@ -16,7 +16,7 @@
 COLS = 16
 VPIECE = 192
 ZPIECE = 96
-WIDTH = 256
+WIDTH = 512
 PEERS = ((0, 0), (0, 1), (1, 0), (0, 3), (3, 0), (1, 1), (3, 3), (1, 3), (3, 1), (0, 2), (2, 0),
          (2, 1), (1, 2), (2, 3), (3, 2), (2, 2))
 MESH = pl.DeviceIdType.MESH
@@ -140,8 +140,6 @@
 
             lax.fori_loop(0, 12, split, 0)
 
-    split_part(0)
-    split_part(1)
     pl.semaphore_wait(bar, COLS - 1 + ROWS - 1)
 
     vtile = 2 * row + col // 8
@@ -211,9 +209,11 @@
                         act(vz.at[src], vbuf.at[slot, rows], vf_send.at[j, i], v_recv.at[slot],
                             row, c, row, col)
 
-    def v_other_each(act, before, first_j=0, last_j=ROWS):
-        for j, step in list(enumerate(((0, 0),) + LINE))[first_j:last_j]:
-            src = line_row(step)
+    def v_other_each(act, before):
+        def one(j, carry):
+            q = lax.rem(j + vpiece, ROWS)
+            steps = ((0, 0),) + LINE
+            src = line_row((choose(q, [p[0] for p in steps]), choose(q, [p[1] for p in steps])))
             tile = 2 * src + parity
 
             @pl.when(jnp.logical_and(tile <= far, src != lead_src))
@@ -222,25 +222,30 @@
 
             @pl.when(tile < row)
             def _():
-                act(vec if j == 0 else vline.at[src], vbuf.at[1, v_rows], vo_send.at[j, 0], v_recv.at[1],
+                act(vline.at[src], vbuf.at[1, v_rows], vo_send.at[q, 0], v_recv.at[1],
                     row, tile, row, col)
 
             @pl.when(tile < far)
             def _():
-                act(vec if j == 0 else vline.at[src], vbuf.at[1, v_rows], vo_send.at[j, 1], v_recv.at[1],
+                act(vline.at[src], vbuf.at[1, v_rows], vo_send.at[q, 1], v_recv.at[1],
                     row, tile + row + 1, row, col)
 
-    v_other_each(put, lambda src: arrived(vline.at[src], vl_recv.at[src]), 0, 1)
+            return carry
+
+        lax.fori_loop(0, ROWS, one, 0)
+
+    split_part(0)
     arrived(vline.at[lead_src], vl_recv.at[lead_src])
     v_lead_each(put)
     v_line_each(lambda copy: copy.start())
     v_hand_each(put, lambda src: arrived(vz.at[src], vz_recv.at[src]))
-    v_other_each(put, lambda src: arrived(vline.at[src], vl_recv.at[src]), 1)
+    v_other_each(put, lambda src: arrived(vline.at[src], vl_recv.at[src]))
 
     @pl.when(jnp.logical_and(vtile > far, lead_src != row))
     def _():
         arrived(vline.at[row], vl_recv.at[row])
 
+    split_part(1)
     split_part(2)
     split_part(3)
 
@@ -437,8 +442,9 @@
             slot = jnp.where(c == row, 1, 0)
             act(zsum.at[half], zf.at[slot, pl.ds(col * ZPIECE, ZPIECE)], z_send.at[0, j],
                 z_recv.at[slot, z_at], row, c, row, col)
-            to = lax.rem(row + sign * j + 2 * ROWS, ROWS)
-            first = j < ROWS
+            n = lax.rem(j + col, COLS)
+            to = lax.rem(row + n, ROWS)
+            first = n < ROWS
             half = jnp.where(jnp.logical_or(first, to > row), 0, 1)
             slot = jnp.where(jnp.logical_or(first, to != row), 1, 0)
             to_col = jnp.where(
@@ -500,11 +506,6 @@
 
         lax.fori_loop(0, 2, one, 0)
 
-    for step in (0, 1, 3, 2):
-        w_into(step)
-
-    arrived(d_out, d_recv)
-
     v_line_lead(lambda copy: copy.wait_send())
     v_line_each(lambda copy: copy.wait_send())
     v_lead_each(sent)
@@ -514,21 +515,32 @@
     z_put(1, sent)
     l_each(lambda copy: copy.wait_send())
 
-    zf_each(0, COLS, sent)
-
-    def all_sent(j, carry):
+    def row_sent(j, carry):
         sent(g1s, g1s, g_send.at[0, j], None, row, j, row, col)
         sent(g2s, g2s, g_send.at[2, j], None, row, j, row, col)
-        sent(dmine, dmine, d_send.at[j], None, row, j, row, col)
-        return carry
-
-    lax.fori_loop(0, 16, all_sent, 0)
+        return carry
+
+    lax.fori_loop(0, COLS, row_sent, 0)
 
     def line_sent(j, carry):
         sent(g1s, g1s, g_send.at[1, j], None, j, col, row, col)
         return carry
 
     lax.fori_loop(0, ROWS, line_sent, 0)
+
+    w_into(0)
+    w_into(1)
+    w_into(3)
+    zf_each(0, COLS, sent)
+
+    def d_sent(j, carry):
+        sent(dmine, dmine, d_send.at[j], None, row, j, row, col)
+        return carry
+
+    lax.fori_loop(0, COLS, d_sent, 0)
+    w_into(2)
+
+    arrived(d_out, d_recv)
 
     for s in range(2):
         for k in range(4):

time: 105 us -> 102 us (0.971)
  Pallas kernels: 104 us -> 101 us
    pallas_call x1, Pallas kernels: 91.5 us -> 89.7 us  [body(): pl.pallas_call(exchange, name='exchange', out_shape=(jax.ShapeDtypeStruct...]
where the time goes in v5:
time: 102 us
  Pallas kernels  101 us (99%)
    pallas_call x1, Pallas kernels, body(): pl.pallas_call(exchange, name='exchange', out_shape=(jax.ShapeDtypeStruct...  89.7 us
    pallas_call x1, Pallas kernels, body(): pl.pallas_call(update, name='update', out_shape=(jax.ShapeDtypeStruct((TI...  11.5 us

profile of v5, /device:TPU:0, one launch (start us, length us, event | category | flops | bytes accessed | tf_op | source)
XLA Modules:
  0.0 102.0 jit_solution(13177572803647293642)
XLA Ops:
  0.6 89.7 %exchange.1 = (bf16[2,1536,512]{2,1,0:T(8,128)(2,1)}, f32[16,8,128]{2,1,0:T(8,128)}) custom-call(f32[1536,1536]{1,0:T(8,128)} %mat.3, f32[1,1536]{1,0:T(1,128)} %fard.1, f32[192,128]{1,0:T(8,128)} %vec.1, f32[128,128]{1,0:T(8,128)} %fac.1), custom_call_target="tpu_custom_call" | custom-call | tf_op jit(solution)/shard_map/exchange/pallas_call | solution.py:631
  90.4 11.5 %update.1 = (f32[1536,1536]{1,0:T(8,128)}, f32[1,1536]{1,0:T(1,128)}) custom-call(f32[1536,1536]{1,0:T(8,128)} %mat.3, bf16[2,1536,512]{2,1,0:T(8,128)(2,1)} %get-tuple-element.4.x_hbm, f32[16,8,128]{2,1,0:T(8,128)} %get-tuple-element.5.d, f32[1,1536]{1,0:T(1,128)} %fard.1), custom_call_target="tpu_custom_call" | custom-call | tf_op jit(solution)/shard_map/update/pallas_call | solution.py:689

commit v6 on v5

--- a/solution.py
+++ b/solution.py
@@ -12,7 +12,7 @@
 GRID = 16
 HALF = 8
 ROWS = 8
-LINE = ((0, 1), (1, 0), (3, 0), (1, 1), (3, 1), (2, 0), (2, 1))
+LINE = ((2, 0), (2, 1), (1, 1), (3, 1), (1, 0), (3, 0), (0, 1))
 COLS = 16
 VPIECE = 192
 ZPIECE = 96
@@ -338,10 +338,10 @@
         part = times_t(vtc[0], bhi[second, :, at], blo[second, :, at])
         zt[:, at] = part
         z[1, at, :] = part.T
-        z_put(1, half=k)
         return carry
 
     lax.fori_loop(0, 2, turned_panel, 0)
+    z_put(1)
 
     arrived(vbuf.at[1], v_recv.at[1])
     cat_v(1)

time: 102 us -> 99.2 us (0.973)
  Pallas kernels: 101 us -> 98.1 us
    pallas_call x1, Pallas kernels: 89.7 us -> 86.6 us  [body(): pl.pallas_call(exchange, name='exchange', out_shape=(jax.ShapeDtypeStruct...]
where the time goes in v6:
time: 99.2 us; the launch traced here: 98.9 us
  Pallas kernels  98.1 us (99%)
    pallas_call x1, Pallas kernels, body(): pl.pallas_call(exchange, name='exchange', out_shape=(jax.ShapeDtypeStruct...  86.6 us
    pallas_call x1, Pallas kernels, body(): pl.pallas_call(update, name='update', out_shape=(jax.ShapeDtypeStruct((TI...  11.5 us

profile of v6, /device:TPU:0, one launch (start us, length us, event | category | flops | bytes accessed | tf_op | source)
XLA Modules:
  0.0 98.9 jit_solution(3213735476477609295)
XLA Ops:
  0.6 86.6 %exchange.1 = (bf16[2,1536,512]{2,1,0:T(8,128)(2,1)}, f32[16,8,128]{2,1,0:T(8,128)}) custom-call(f32[1536,1536]{1,0:T(8,128)} %mat.3, f32[1,1536]{1,0:T(1,128)} %fard.1, f32[192,128]{1,0:T(8,128)} %vec.1, f32[128,128]{1,0:T(8,128)} %fac.1), custom_call_target="tpu_custom_call" | custom-call | tf_op jit(solution)/shard_map/exchange/pallas_call | solution.py:631
  87.2 11.5 %update.1 = (f32[1536,1536]{1,0:T(8,128)}, f32[1,1536]{1,0:T(1,128)}) custom-call(f32[1536,1536]{1,0:T(8,128)} %mat.3, bf16[2,1536,512]{2,1,0:T(8,128)(2,1)} %get-tuple-element.4.x_hbm, f32[16,8,128]{2,1,0:T(8,128)} %get-tuple-element.5.d, f32[1,1536]{1,0:T(1,128)} %fard.1), custom_call_target="tpu_custom_call" | custom-call | tf_op jit(solution)/shard_map/update/pallas_call | solution.py:689
